TPU v7x, 512 devices: a whole 4x8x8 slice. The times are simulated.
512 devices in a mesh: seq: 64 (over x, z, core), kvh: 8 (over y).
Axes of the slice: x: 4, y: 8, z: 8, core: 2. Of those that a mesh axis runs over, the one named last changes fastest.
Arguments:
- queries: bfloat16 [128, 2, 64, 128], P('seq', None, 'kvh'), may hold values from -6 to 6
- new_keys: bfloat16 [128, 2, 8, 128], P('seq', None, 'kvh'), may hold values from -12 to 12
- new_values: bfloat16 [128, 2, 8, 128], P('seq', None, 'kvh'), may hold values from -6 to 6
- prefix_keys: bfloat16 [16384, 8, 128], P('seq', 'kvh'), may hold values from -12 to 12
- prefix_values: bfloat16 [16384, 8, 128], P('seq', 'kvh'), may hold values from -6 to 6
- prompt_keys: bfloat16 [32768, 8, 128], P('seq', 'kvh'), may hold values from -12 to 12
- prompt_values: bfloat16 [32768, 8, 128], P('seq', 'kvh'), may hold values from -6 to 6
- cache_keys: bfloat16 [128, 256, 8, 128], P('seq', None, 'kvh'), may hold values from -12 to 12
- cache_values: bfloat16 [128, 256, 8, 128], P('seq', None, 'kvh'), may hold values from -6 to 6
- group_prompt: int32 [16], replicated, may hold values from 0 to 15, each once
- prompt_len: int32 [16], replicated, may hold values from 256 to 2048, as said below
- cont_prompt: int32 [128], replicated, may hold values from 0 to 15, as said below
- cont_len: int32 [128], P('seq'), may hold values from 1 to 256, as said below
- out_weight: bfloat16 [8192, 5120], P('kvh', 'seq'), may hold values from -0.0625 to 0.0625
Outputs:
- output: float32 [128, 2, 5120], P('kvh', None, 'seq')
Inputs may be any that keep to these rules, and one draw needn't show every extreme that they name: `cont_prompt`: every prompt has exactly 8 continuations. `prompt_len`: the longest prompt has exactly 2048 tokens and the shortest 2048 // 8. `cont_len`: some continuation uses all 256 cache rows and some only one.
All inputs are finite; a program needn't handle non-finite values.
Results may differ from a plain program's by a relative error of at most 0.0021.
The roundings to bfloat16 on the way count: a program that leaves them out, or rounds other values in their place, can miss the bound.
Values may be sent and summed in bfloat16 or wider, within the bound.
A program may use at most 192 MiB of HBM per device.

v0:
```python
import math

import jax
import jax.numpy as jnp
from jax import lax
from jax.sharding import PartitionSpec as P

NEG = -1e30


def block_partial(query_rows, key_rows, value_rows, usable, scaling):
    scores = jnp.dot(query_rows, key_rows.T, preferred_element_type=jnp.float32) * scaling
    scores = jnp.where(usable, scores, NEG)
    maximum = jnp.max(scores, axis=-1)
    weights = jnp.where(usable, jnp.exp(scores - maximum[..., None]), 0.0).astype(jnp.bfloat16)
    weights = lax.optimization_barrier(weights)
    totals = jnp.sum(weights.astype(jnp.float32), axis=-1)
    weighted = jnp.dot(weights, value_rows, preferred_element_type=jnp.float32)
    return (maximum, totals, weighted)


def join_partials(former, latter):
    maximum = jnp.maximum(former[0], latter[0])
    former_scale = jnp.exp(former[0] - maximum)
    latter_scale = jnp.exp(latter[0] - maximum)
    return (
        maximum,
        former[1] * former_scale + latter[1] * latter_scale,
        former[2] * former_scale[..., None] + latter[2] * latter_scale[..., None],
    )


def prompt_partial(
    all_queries,
    key_rows,
    value_rows,
    device,
    group_prompt,
    prompt_len,
    cont_prompt,
    group_span,
    per_prompt,
    scaling,
):
    cont_count, fresh_count, group_size, head_width = all_queries.shape
    prompts = group_prompt.shape[0]
    slot_ids = jnp.arange(prompts, dtype=jnp.int32)
    owned = jnp.sum(jnp.where(slot_ids == device // group_span, group_prompt, 0))
    length = jnp.sum(jnp.where(slot_ids == owned, prompt_len, 0))
    chosen = jnp.nonzero(cont_prompt == owned, size=per_prompt)[0].astype(jnp.int32)
    picked = all_queries[chosen].reshape(per_prompt * fresh_count * group_size, head_width)
    span_len = key_rows.shape[0]
    places = device % group_span * span_len + jnp.arange(span_len, dtype=jnp.int32)
    maximum, totals, weighted = block_partial(
        picked, key_rows, value_rows, (places < length)[None, :], scaling
    )
    shape3 = (per_prompt, fresh_count, group_size)
    full_max = (
        jnp.full((cont_count, fresh_count, group_size), NEG, jnp.float32)
        .at[chosen]
        .set(maximum.reshape(shape3))
    )
    full_tot = (
        jnp.zeros((cont_count, fresh_count, group_size), jnp.float32)
        .at[chosen]
        .set(totals.reshape(shape3))
    )
    full_wtd = (
        jnp.zeros((cont_count, fresh_count, group_size, head_width), jnp.float32)
        .at[chosen]
        .set(weighted.reshape(shape3 + (head_width,)))
    )
    return (full_max, full_tot, full_wtd)


def own_partial(local_queries, cache_k, cache_v, fresh_k, fresh_v, lengths, scaling):
    cont_count, fresh_count, group_size, head_width = local_queries.shape
    gen_len = cache_k.shape[1]
    past = jnp.einsum("ctgd,cjd->ctgj", local_queries, cache_k, preferred_element_type=jnp.float32)
    recent = jnp.einsum(
        "ctgd,cud->ctgu", local_queries, fresh_k, preferred_element_type=jnp.float32
    )
    scores = jnp.concatenate([past, recent], axis=3) * scaling
    usable_past = jnp.arange(gen_len, dtype=jnp.int32)[None, :] < lengths[:, None]
    usable_new = (
        jnp.arange(fresh_count, dtype=jnp.int32)[None, :]
        <= jnp.arange(fresh_count, dtype=jnp.int32)[:, None]
    )
    usable = jnp.concatenate(
        [
            jnp.broadcast_to(usable_past[:, None, None, :], (cont_count, fresh_count, 1, gen_len)),
            jnp.broadcast_to(
                usable_new[None, :, None, :], (cont_count, fresh_count, 1, fresh_count)
            ),
        ],
        axis=3,
    )
    scores = jnp.where(usable, scores, NEG)
    maximum = jnp.max(scores, axis=-1)
    weights = jnp.where(usable, jnp.exp(scores - maximum[..., None]), 0.0).astype(jnp.bfloat16)
    weights = lax.optimization_barrier(weights)
    totals = jnp.sum(weights.astype(jnp.float32), axis=-1)
    weighted = jnp.einsum(
        "ctgj,cjd->ctgd", weights[..., :gen_len], cache_v, preferred_element_type=jnp.float32
    )
    weighted = weighted + jnp.einsum(
        "ctgu,cud->ctgd", weights[..., gen_len:], fresh_v, preferred_element_type=jnp.float32
    )
    return (maximum, totals, weighted)


def body(
    queries,
    new_keys,
    new_values,
    prefix_keys,
    prefix_values,
    prompt_keys,
    prompt_values,
    cache_keys,
    cache_values,
    group_prompt,
    prompt_len,
    cont_prompt,
    cont_len,
    out_weight,
):
    own_count, fresh_count, local_query_heads, head_width = queries.shape
    local_heads = prefix_keys.shape[1]
    group_size = local_query_heads // local_heads
    seq_count = lax.axis_size("seq")
    seq_index = lax.axis_index("seq")
    prompts = group_prompt.shape[0]
    cont_count = own_count * seq_count
    per_prompt = cont_count // prompts
    group_span = seq_count // prompts
    scaling = 1.0 / math.sqrt(head_width)
    gathered = lax.all_gather(queries, "seq", axis=0, tiled=True)
    shape3 = (cont_count, fresh_count, group_size)
    offset = seq_index * own_count
    query_rows = gathered.reshape(-1, head_width)
    row_total = query_rows.shape[0]
    pieces = max(1, row_total // 1024)
    while row_total % pieces:
        pieces -= 1
    prefix_k = prefix_keys[:, 0, :]
    prefix_v = prefix_values[:, 0, :]
    every_key = jnp.ones((1, prefix_k.shape[0]), dtype=bool)

    def prefix_piece(blocked):
        return block_partial(blocked, prefix_k, prefix_v, every_key, scaling)

    maximum, totals, weighted = lax.map(
        prefix_piece, query_rows.reshape(pieces, row_total // pieces, head_width)
    )
    prefix_part = (
        maximum.reshape(shape3),
        totals.reshape(shape3),
        weighted.reshape(shape3 + (head_width,)),
    )
    prompt_part = prompt_partial(
        gathered,
        prompt_keys[:, 0, :],
        prompt_values[:, 0, :],
        seq_index,
        group_prompt,
        prompt_len,
        cont_prompt,
        group_span,
        per_prompt,
        scaling,
    )
    own_part = own_partial(
        queries,
        cache_keys[:, :, 0, :],
        cache_values[:, :, 0, :],
        new_keys[:, :, 0, :],
        new_values[:, :, 0, :],
        cont_len,
        scaling,
    )
    own_full = (
        lax.dynamic_update_slice_in_dim(jnp.full(shape3, NEG, jnp.float32), own_part[0], offset, 0),
        lax.dynamic_update_slice_in_dim(jnp.zeros(shape3, jnp.float32), own_part[1], offset, 0),
        lax.dynamic_update_slice_in_dim(
            jnp.zeros(shape3 + (head_width,), jnp.float32), own_part[2], offset, 0
        ),
    )
    head_parts = [join_partials(join_partials(prefix_part, prompt_part), own_full)]
    combined = (
        jnp.concatenate([entry[0] for entry in head_parts], axis=2),
        jnp.concatenate([entry[1] for entry in head_parts], axis=2),
        jnp.concatenate([entry[2] for entry in head_parts], axis=2),
    )
    overall = lax.pmax(combined[0], "seq")
    factors = jnp.exp(combined[0] - overall)
    weighted_own, totals_own = (
        lax.psum_scatter(combined[2] * factors[..., None], "seq", scatter_dimension=0, tiled=True),
        lax.psum_scatter(combined[1] * factors, "seq", scatter_dimension=0, tiled=True),
    )
    attn_own = (weighted_own / totals_own[..., None]).astype(jnp.bfloat16)
    attention = lax.all_gather(attn_own, "seq", axis=0, tiled=True)
    flat = attention.reshape(cont_count * fresh_count, local_query_heads * head_width)
    projected = jnp.dot(flat, out_weight, preferred_element_type=jnp.float32).reshape(
        cont_count, fresh_count, -1
    )
    return lax.psum_scatter(projected, "kvh", scatter_dimension=0, tiled=True)


def solution(mesh):
    in_specs = (
        P("seq", None, "kvh", None),
        P("seq", None, "kvh", None),
        P("seq", None, "kvh", None),
        P("seq", "kvh", None),
        P("seq", "kvh", None),
        P("seq", "kvh", None),
        P("seq", "kvh", None),
        P("seq", None, "kvh", None),
        P("seq", None, "kvh", None),
        P(),
        P(),
        P(),
        P("seq"),
        P("kvh", "seq"),
    )
    out_specs = P("kvh", None, "seq")
    return jax.shard_map(body, mesh=mesh, in_specs=in_specs, out_specs=out_specs, check_vma=False)
```

profile of v0, /device:TPU:1, one launch (start us, length us, event | category | flops | bytes accessed | tf_op | source)
XLA Modules:
  0.0 546.8 jit_solution(12447309896419600487)
XLA Ops:
  6.5 0.7 copy-done.10
  7.2 0.6 fusion.24
  7.9 0.6 fusion.28
  8.6 1.3 fusion.29
  9.9 57.8 %all_gather.6 = bf16[128,2,8,128]{3,2,1,0:T(8,128)(2,1)S(1)} all-gather(bf16[2,2,8,128]{3,2,1,0:T(8,128)(2,1)S(1)} %copy-done.7), channel_id=1, replica_groups=mesh['seq'=64,'kvh'=8] {'seq'}, dimensions={0}, use_global_device_ids=true | all-gather | bytes 532480 | tf_op jit(solution)/shard_map/all_gather | solution.py:138
  67.7 0.1 fusion.10
  67.8 0.5 copy-done.8
  68.4 0.1 fusion.22
  68.5 0.5 copy-done.12
  69.1 0.1 fusion.17
  69.4 0.1 copy.91
  69.5 0.2 reduce-window.6
  69.7 0.1 fusion.15
  69.8 1.4 scatter_custom_fusion
  71.2 0.2 select_n.98
  71.4 0.6 fusion.27
  72.0 0.6 copy-done.13
  72.7 1.3 fusion.25
  73.9 0.6 gather_fusion
  74.5 0.6 add_compare_fusion
  75.1 0.3 fusion.34
  75.3 0.1 reshape.187
  75.5 0.7 scatter_fusion
  76.3 0.8 copy-done.1
  77.1 2.1 while.14
  77.1 0.3 fusion.51
  77.4 0.2 exponential_convert_fusion.2
  77.6 0.4 fusion.52
  78.0 0.1 convert_reduce_fusion.4
  78.2 0.3 fusion.51
  78.5 0.2 exponential_convert_fusion.2
  78.7 0.4 fusion.52
  79.0 0.1 convert_reduce_fusion.4
  79.3 0.2 reshape.160
  79.6 0.4 dynamic_update_slice.20
  80.0 125.4 %pmax.7 = f32[128,2,8]{0,2,1:T(8,128)S(1)} all-reduce(f32[128,2,8]{0,2,1:T(8,128)S(1)} %get-tuple-element.67), channel_id=1, replica_groups=mesh['seq'=64,'kvh'=8] {'seq'}, use_global_device_ids=true, to_apply=%region_14.15 | all-reduce | flops 2048 | bytes 16384 | tf_op jit(solution)/shard_map/pmax | solution.py:195
  205.4 0.1 select_convert_fusion
  205.5 0.1 convert_reduce_fusion.1
  205.6 0.1 reshape.203
  205.7 0.7 scatter_fusion.2
  206.7 0.3 reshape.165
  207.0 0.4 dynamic_update_slice.22
  207.5 0.1 copy.101
  207.6 0.1 copy.103
  207.8 0.1 copy.104
  207.9 0.1 copy.96
  208.1 0.1 copy.98
  208.2 0.6 copy-done.3
  208.8 0.1 fusion.8
  209.0 0.2 fusion.12
  209.3 0.7 scatter_fusion.1
  210.1 0.6 copy-done.9
  210.7 0.1 fusion.5
  210.8 1.7 add_multiply_fusion
  212.5 1.1 copy.105
  213.7 0.1 copy.110
  213.8 1.3 dynamic-slice
  215.7 244.0 %all-reduce.1 = f32[128,2,8]{2,1,0:T(2,128)S(1)} all-reduce(f32[128,2,8]{2,1,0:T(2,128)S(1)} %copy.110), channel_id=3, replica_groups=mesh['seq'=64,'kvh'=8] {'seq'}, use_global_device_ids=true, to_apply=%region_19.20.clone | all-reduce | flops 2048 | bytes 16384
  459.7 0.8 fusion.19
  460.5 46.5 %all_gather.7 = bf16[128,2,8,128]{3,2,0,1:T(8,128)(2,1)S(1)} all-gather(bf16[2,2,8,128]{3,2,0,1:T(8,128)(2,1)S(1)} %fusion.19), channel_id=1, replica_groups=mesh['seq'=64,'kvh'=8] {'seq'}, dimensions={0}, use_global_device_ids=true | all-gather | bytes 532480 | tf_op jit(solution)/shard_map/all_gather | solution.py:202
  507.0 0.2 dot_general.38
  507.3 0.9 fusion.6
  508.2 30.4 %reduce-scatter.3.cloned.1.call-done = f32[16,2,80]{2,0,1:T(8,128)} async-done(((f32[128,2,80]{2,0,1:T(8,128)}), f32[16,2,80]{2,0,1:T(8,128)}) %reduce-scatter.3.cloned.1.call-update) | async-done | bytes 10256 | tf_op jit(solution)/shard_map/reduce_scatter | solution.py:207
  538.6 1.3 copy.112
  (58 shorter events, 1.4 us)
Async XLA Ops:
  6.5 500.7 %copy-start = (bf16[1024,80]{0,1:T(8,128)(2,1)S(1)}, bf16[1024,80]{0,1:T(8,128)(2,1)}, u32[]{:S(2)}) copy-start(bf16[1024,80]{0,1:T(8,128)(2,1)} %param.29) | copy-start | bytes 491524
  6.5 453.2 %all-reduce.4.cloned.1.call-start = ((), (), s32[]{:S(2)}) async-start(), calls=%async_computation.2 | async-start | bytes 2097152
  6.5 0.7 copy-start.10
  7.2 0.7 copy-start.11
  8.5 1.3 copy-start.7
  9.8 57.8 %copy-start.4 = (bf16[2,256,1,128]{3,1,2,0:T(8,128)(2,1)S(1)}, bf16[2,256,1,128]{3,1,2,0:T(8,128)(2,1)}, u32[]{:S(2)}) copy-start(bf16[2,256,1,128]{3,1,2,0:T(8,128)(2,1)} %param.23) | copy-start | bytes 393220
  67.7 0.7 copy-start.8
  68.3 0.7 copy-start.12
  69.5 5.6 %copy-start.5 = (bf16[512,1,128]{2,0,1:T(8,128)(2,1)S(1)}, bf16[512,1,128]{2,0,1:T(8,128)(2,1)}, u32[]{:S(2)}) copy-start(bf16[512,1,128]{2,0,1:T(8,128)(2,1)} %param.21) | copy-start | bytes 393220
  72.0 0.7 copy-start.13
  76.2 0.8 copy-start.1
  76.2 0.9 copy-start.2
  207.9 0.9 copy-start.3
  208.1 0.9 copy-start.6
  210.0 0.7 copy-start.9
  213.6 325.0 %reduce-scatter.3.cloned.1.call-start = ((), (), s32[]{:S(2)}) async-start(), calls=%async_computation.1 | async-start | bytes 147456 | tf_op jit(solution)/shard_map/reduce_scatter | solution.py:207
Sparse Core Ops, SparseCore 0:
  213.7 192.0 all-reduce.3
  508.3 30.2 reduce-scatter.2
where the time goes:
time: 552 us; the launch traced here: 547 us
  blocking collectives  474 us (86%)
  waiting for transfers between devices  30.4 us (6%)
  local copies, waits for them, and re-layouts  14.5 us (3%)
  between operations  14.4 us (3%)
  other arithmetic  10.5 us (2%)
    unnamed x1, blocking collectives  244 us
    pmax x1, blocking collectives, body(): overall = lax.pmax(combined[0], 'seq')  125 us
    all_gather x1, blocking collectives, body(): gathered = lax.all_gather(queries, 'seq', axis=0, tiled=True)  57.8 us
    all_gather x1, blocking collectives, body(): attention = lax.all_gather(attn_own, 'seq', axis=0, tiled=True)  46.5 us
    reduce_scatter x1, waiting for transfers between devices, body(): return lax.psum_scatter(projected, 'kvh', scatter_dimension=0, tiled=True)  30.4 us
  transfers between devices with their start and end apart: 2, of which 1 were waited for; matrix products, arithmetic and copies ran while one was open for 0% of the time, Pallas kernels for 0%

commit v1 on v0

v1 whole, which is shorter than its diff:
```python
import functools
import math

import jax
import jax.numpy as jnp
from jax import lax
from jax.experimental import pallas as pl
from jax.experimental.pallas import tpu as pltpu
from jax.sharding import PartitionSpec as P

NEG = -1e30
MESH = pl.DeviceIdType.MESH
F32, BF16 = jnp.float32, jnp.bfloat16
NX, NZ, NC, NY = 4, 8, 2, 8
CHIPS = NX * NZ
ROWS = 32
HD = 128
GROUP = 8
SCALING = 1.0 / math.sqrt(HD)


def dot(a, b):
    return jnp.dot(a, b, preferred_element_type=F32)


def dot_nt(a, b):
    return lax.dot_general(a, b, (((1,), (1,)), ((), ())), preferred_element_type=F32)


def iota(shape, axis):
    return lax.broadcasted_iota(jnp.int32, shape, axis)


def loop(low, high, step):
    def run(k, carry):
        step(k)
        return carry

    lax.fori_loop(low, high, run, 0)


def remote(src, dst, send_sem, recv_sem, chip, y, core):
    return pltpu.make_async_remote_copy(
        src_ref=src,
        dst_ref=dst,
        send_sem=send_sem,
        recv_sem=recv_sem,
        device_id={"seq": chip * 2 + core, "kvh": y},
        device_id_type=MESH,
    )


def with_ones(values):
    flipped = jnp.transpose(values.astype(F32))
    return jnp.concatenate([flipped, jnp.ones((16, values.shape[0]), F32)], axis=0).astype(BF16)


def kernel(
    q_in,
    pk_in,
    pv_in,
    sk_in,
    sv_in,
    ck_in,
    cv_in,
    w_in,
    nk_ref,
    nv_ref,
    cont_prompt_ref,
    group_prompt_ref,
    prompt_len_ref,
    cont_len_ref,
    out_ref,
    q_all,
    pk,
    pv,
    sk,
    sv,
    ck,
    cv,
    wt,
    pvt,
    svt,
    member,
    x_send,
    x_recv,
    z_send,
    z_recv,
    att,
    att_f32,
    flat,
    y_send,
    y_recv,
    own_sem,
    swap_ss,
    swap_rs,
    q_ss,
    q_rs,
    x_ss,
    x_rs,
    z_ss,
    z_rs,
    a_ss,
    a_rs,
    y_ss,
    y_rs,
):
    seq = lax.axis_index("seq")
    y = lax.axis_index("kvh")
    chip, c = seq // 2, seq % 2
    x, z = chip // NZ, chip % NZ
    other = 1 - c
    yc = y * 2 + c

    barrier = pltpu.get_barrier_semaphore()

    def greet_plane(k):
        pl.semaphore_signal(
            barrier,
            inc=1,
            device_id={"seq": lax.rem(chip + k, CHIPS) * 2 + c, "kvh": y},
            device_id_type=MESH,
        )

    def greet_column(k):
        to = lax.rem(yc + k, 16)
        pl.semaphore_signal(
            barrier, inc=1, device_id={"seq": chip * 2 + to % 2, "kvh": to // 2}, device_id_type=MESH
        )

    loop(1, CHIPS, greet_plane)
    loop(1, 16, greet_column)

    local = [
        pltpu.make_async_copy(src, dst, own_sem.at[n])
        for n, (src, dst) in enumerate(
            [
                (q_in, q_all.at[chip]),
                (ck_in, ck),
                (cv_in, cv),
                (pk_in, pk.at[c]),
                (pv_in, pv.at[c]),
                (sk_in, sk.at[c]),
                (sv_in, sv.at[c]),
                (w_in, wt.at[c, pl.ds(0, 80)]),
            ]
        )
    ]
    for copy in local:
        copy.start()
    wt[:, 80:, :] = jnp.zeros((2, 48, wt.shape[2]), BF16)
    for copy in local[:3]:
        copy.wait()

    q_own = q_all[chip]
    first = iota((ROWS, 1), 0) < 16
    past0 = dot_nt(q_own, ck[0]) * SCALING
    past1 = dot_nt(q_own, ck[1]) * SCALING
    lengths = jnp.where(first, cont_len_ref[0], cont_len_ref[1])
    past = jnp.where(iota(past0.shape, 1) < lengths, jnp.where(first, past0, past1), NEG)
    fresh_pad = jnp.zeros((12, HD), F32)
    nk = jnp.concatenate([nk_ref[0].astype(F32), nk_ref[1].astype(F32), fresh_pad], axis=0).astype(BF16)
    nv = jnp.concatenate([nv_ref[0].astype(F32), nv_ref[1].astype(F32), fresh_pad], axis=0).astype(BF16)
    fresh = dot_nt(q_own, nk) * SCALING
    row, col = iota(fresh.shape, 0), iota(fresh.shape, 1)
    seen = (col // 2 == row // 16) & (col % 2 <= (row // 8) % 2)
    fresh = jnp.where(seen, fresh, NEG)
    own_peak = jnp.maximum(jnp.max(past, axis=1, keepdims=True), jnp.max(fresh, axis=1, keepdims=True))
    past_w = jnp.exp(past - own_peak).astype(BF16)
    fresh_w = jnp.exp(fresh - own_peak).astype(BF16)
    own_total = jnp.sum(past_w.astype(F32), axis=1, keepdims=True) + jnp.sum(
        fresh_w.astype(F32), axis=1, keepdims=True
    )
    own_part = jnp.where(first, dot(past_w, cv[0]), dot(past_w, cv[1])) + dot(fresh_w, nv)

    prompt = group_prompt_ref[chip // 2]
    length = prompt_len_ref[prompt]
    prompts = jnp.broadcast_to(cont_prompt_ref[...].astype(F32), (8, 128)).astype(BF16)
    for g in range(NX):
        lane = iota((128, 256), 1)
        cont = (g * NZ + lane // ROWS) * 4 + c * 2 + (lane % ROWS) // 16
        spread = jnp.where(iota((128, 256), 0) == cont, 1.0, 0.0).astype(BF16)
        prompt_of = dot(prompts, spread)
        member[g] = jnp.where(prompt_of == jnp.full((8, 256), prompt, jnp.int32).astype(F32), 1.0, 0.0)

    pl.semaphore_wait(barrier, CHIPS - 1 + 15)

    def q_copy(k):
        block = q_all.at[chip]
        return remote(block, block, q_ss.at[k], q_rs.at[k], lax.rem(chip + k, CHIPS), y, c)

    loop(1, CHIPS, lambda k: q_copy(k).start())
    swaps = [
        remote(src, dst, swap_ss.at[n], swap_rs.at[n], chip, y, other)
        for n, (src, dst) in enumerate(
            [
                (pk_in, pk.at[c]),
                (pv_in, pv.at[c]),
                (sk_in, sk.at[c]),
                (sv_in, sv.at[c]),
                (w_in, wt.at[c, pl.ds(0, 80)]),
            ]
        )
    ]
    for copy in swaps:
        copy.start()
    for copy in local[3:]:
        copy.wait()
    pvt[c] = with_ones(pv[c])
    svt[c] = with_ones(sv[c])
    for copy in swaps:
        copy.wait_recv()
    pvt[other] = with_ones(pv[other])
    svt[other] = with_ones(sv[other])

    def group_partial(g, put):
        rows = q_all[pl.ds(g * NZ, NZ)].reshape(NZ * ROWS, HD)
        mine = member[g][0:1] > 0.5
        peaks, parts = [], []
        for b in range(2):
            scores = dot_nt(pk[b], rows) * SCALING
            peak = jnp.max(scores, axis=0, keepdims=True)
            weights = jnp.exp(scores - peak).astype(BF16)
            peaks.append(peak)
            parts.append(dot(pvt[b], weights))
        for b in range(2):
            scores = dot_nt(sk[b], rows) * SCALING
            place = ((z % 2) * 2 + b) * 512 + iota((512, 1), 0)
            scores = jnp.where(place < length, scores, NEG)
            peak = jnp.max(scores, axis=0, keepdims=True)
            weights = jnp.exp(scores - peak).astype(BF16)
            peaks.append(jnp.where(mine, peak, NEG))
            parts.append(dot(svt[b], weights))
        put(*join(peaks, parts))

    def join(peaks, parts):
        top = functools.reduce(jnp.maximum, peaks)
        total = None
        for peak, part in zip(peaks, parts):
            term = jnp.exp(peak - top) * part[0:136]
            total = term if total is None else total + term
        stats = jnp.where(iota((8, 256), 0) == 1, top, total[128:136])
        return total[0:128], stats

    def x_copy(k):
        to = lax.rem(x + k, NX)
        return remote(x_send.at[to], x_recv.at[x], x_ss.at[k], x_rs.at[k], to * NZ + z, y, c)

    def q_wait(g):
        def one(n):
            k = lax.rem(chip - (g * NZ + n) + CHIPS, CHIPS)

            @pl.when(k > 0)
            def _():
                q_copy(k).wait_recv()

        loop(0, NZ, one)

    def group_step(k):
        g = lax.rem(x + k, NX)
        q_wait(g)

        def put_send(part, stats):
            x_send[g, 0:128] = part
            x_send[g, 128:136] = stats

        group_partial(g, put_send)
        x_copy(k).start()

    loop(1, NX, group_step)
    q_wait(x)

    def put_own(part, stats):
        x_recv[x, 0:128] = part
        x_recv[x, 128:136] = stats

    group_partial(x, put_own)
    loop(1, NX, lambda k: x_copy(k).wait_recv())

    part, stats = join([x_recv[s, 129:130] for s in range(NX)], [x_recv[s] for s in range(NX)])
    by_row = jnp.transpose(part)
    for t in range(NZ):
        half = stats[:, (t // 4) * 128 : (t // 4 + 1) * 128]
        turned = half if t % 4 == 0 else pltpu.roll(half, 128 - (t % 4) * ROWS, 1)
        z_send[t, 0:ROWS] = by_row[t * ROWS : (t + 1) * ROWS]
        z_send[t, ROWS : ROWS + 8] = turned
    z_recv[z] = z_send[z]

    def z_copy(k):
        to = lax.rem(z + k, NZ)
        return remote(z_send.at[to], z_recv.at[z], z_ss.at[k], z_rs.at[k], x * NZ + to, y, c)

    loop(1, NZ, lambda k: z_copy(k).start())
    loop(1, NZ, lambda k: z_copy(k).wait_recv())

    side = jnp.concatenate(
        [z_recv[s, ROWS + 1 : ROWS + 2] for s in range(NZ)]
        + [z_recv[s, ROWS : ROWS + 1] for s in range(NZ)]
        + [jnp.zeros((112, 128), F32)],
        axis=0,
    )
    side = jnp.transpose(side)[0:ROWS]
    top = jnp.maximum(jnp.max(side[:, 0:NZ], axis=1, keepdims=True), own_peak)
    own_factor = jnp.exp(own_peak - top)
    total, weighted = own_factor * own_total, own_factor * own_part
    for s in range(NZ):
        factor = jnp.exp(side[:, s : s + 1] - top)
        total = total + factor * side[:, NZ + s : NZ + s + 1]
        weighted = weighted + factor * z_recv[s, 0:ROWS]
    att[chip] = (weighted / total).astype(BF16)

    def a_copy(k):
        block = att.at[chip]
        return remote(block, block, a_ss.at[k], a_rs.at[k], lax.rem(chip + k, CHIPS), y, c)

    loop(1, CHIPS, lambda k: a_copy(k).start())
    loop(1, CHIPS, lambda k: a_copy(k).wait_recv())

    att_f32[...] = att[...].reshape(CHIPS * ROWS, HD).astype(F32)
    for h in range(GROUP):
        flat[:, h * HD : (h + 1) * HD] = att_f32[pl.ds(h, 128, stride=GROUP), :].astype(BF16)
    for b in range(2):
        y_send[b] = dot_nt(flat[...], wt[b]).reshape(NY, 16, 128)
    y_recv[yc] = y_send[c, y]

    def y_copy(k):
        to = lax.rem(yc + k, 16)
        return remote(
            y_send.at[to % 2, to // 2], y_recv.at[yc], y_ss.at[k], y_rs.at[k], chip, to // 2, to % 2
        )

    loop(1, 16, lambda k: y_copy(k).start())
    loop(1, 16, lambda k: y_copy(k).wait_recv())
    for b in range(2):
        summed = functools.reduce(jnp.add, [y_recv[n * 2 + b] for n in range(NY)])
        for n in range(4):
            for i in range(2):
                out_ref[n * 4 + b * 2 + i] = summed[n * 4 + i * 2 : n * 4 + i * 2 + 2, 0:80]

    for copy in swaps:
        copy.wait_send()
    loop(1, CHIPS, lambda k: q_copy(k).wait_send())
    loop(1, NX, lambda k: x_copy(k).wait_send())
    loop(1, NZ, lambda k: z_copy(k).wait_send())
    loop(1, CHIPS, lambda k: a_copy(k).wait_send())
    loop(1, 16, lambda k: y_copy(k).wait_send())


def body(
    queries,
    new_keys,
    new_values,
    prefix_keys,
    prefix_values,
    prompt_keys,
    prompt_values,
    cache_keys,
    cache_values,
    group_prompt,
    prompt_len,
    cont_prompt,
    cont_len,
    out_weight,
):
    anywhere = pl.BlockSpec(memory_space=pl.ANY)
    vmem = pl.BlockSpec(memory_space=pltpu.VMEM)
    smem = pl.BlockSpec(memory_space=pltpu.SMEM)
    dma = pltpu.SemaphoreType.DMA
    return pl.pallas_call(
        kernel,
        out_shape=jax.ShapeDtypeStruct((16, 2, 80), F32),
        in_specs=[anywhere] * 8 + [vmem] * 3 + [smem] * 3,
        out_specs=vmem,
        scratch_shapes=[
            pltpu.VMEM((CHIPS, ROWS, HD), BF16),
            pltpu.VMEM((2, 256, HD), BF16),
            pltpu.VMEM((2, 256, HD), BF16),
            pltpu.VMEM((2, 512, HD), BF16),
            pltpu.VMEM((2, 512, HD), BF16),
            pltpu.VMEM((2, 256, HD), BF16),
            pltpu.VMEM((2, 256, HD), BF16),
            pltpu.VMEM((2, 128, 1024), BF16),
            pltpu.VMEM((2, 144, 256), BF16),
            pltpu.VMEM((2, 144, 512), BF16),
            pltpu.VMEM((NX, 8, 256), F32),
            pltpu.VMEM((NX, 136, 256), F32),
            pltpu.VMEM((NX, 136, 256), F32),
            pltpu.VMEM((NZ, 40, 128), F32),
            pltpu.VMEM((NZ, 40, 128), F32),
            pltpu.VMEM((CHIPS, ROWS, HD), BF16),
            pltpu.VMEM((CHIPS * ROWS, HD), F32),
            pltpu.VMEM((128, 1024), BF16),
            pltpu.VMEM((2, NY, 16, 128), F32),
            pltpu.VMEM((16, 16, 128), F32),
            dma((8,)),
            dma((5,)),
            dma((5,)),
            dma((CHIPS,)),
            dma((CHIPS,)),
            dma((NX,)),
            dma((NX,)),
            dma((NZ,)),
            dma((NZ,)),
            dma((CHIPS,)),
            dma((CHIPS,)),
            dma((16,)),
            dma((16,)),
        ],
        compiler_params=pltpu.CompilerParams(
            collective_id=0, has_side_effects=True, vmem_limit_bytes=32 << 20
        ),
    )(
        queries.reshape(ROWS, HD),
        prefix_keys[:, 0, :],
        prefix_values[:, 0, :],
        prompt_keys[:, 0, :],
        prompt_values[:, 0, :],
        cache_keys[:, :, 0, :],
        cache_values[:, :, 0, :],
        out_weight.T,
        new_keys[:, :, 0, :],
        new_values[:, :, 0, :],
        cont_prompt.reshape(1, 128),
        group_prompt,
        prompt_len,
        cont_len,
    )


def solution(mesh):
    in_specs = (
        P("seq", None, "kvh", None),
        P("seq", None, "kvh", None),
        P("seq", None, "kvh", None),
        P("seq", "kvh", None),
        P("seq", "kvh", None),
        P("seq", "kvh", None),
        P("seq", "kvh", None),
        P("seq", None, "kvh", None),
        P("seq", None, "kvh", None),
        P(),
        P(),
        P(),
        P("seq"),
        P("kvh", "seq"),
    )
    out_specs = P("kvh", None, "seq")
    return jax.shard_map(body, mesh=mesh, in_specs=in_specs, out_specs=out_specs, check_vma=False)
```

time: 552 us -> 67 us (0.12)
  blocking collectives: 474 us -> 0 us
  Pallas kernels: 0 us -> 59 us
  waiting for transfers between devices: 30.4 us -> 0 us
  between operations: 14.4 us -> 0.06 us
  other arithmetic: 10.5 us -> 0 us
  local copies, waits for them, and re-layouts: 14.5 us -> 7.54 us
    unnamed x1 -> x0, blocking collectives: 244 us -> none
    pmax x1 -> x0, blocking collectives: 125 us -> none  [body(): overall = lax.pmax(combined[0], 'seq')]
    all_gather x2 -> x0, blocking collectives: 104 us -> none  [the longest x1 57.8 us: body(): gathered = lax.all_gather(queries, 'seq', axis=0, tiled=True)]
    pallas_call x0 -> x1, Pallas kernels: none -> 59 us  [body(): pl.pallas_call(kernel, out_shape=jax.ShapeDtypeStruct((16, 2, 80), F32),...]
    reduce_scatter x1 -> x0, waiting for transfers between devices: 30.4 us -> none  [body(): return lax.psum_scatter(projected, 'kvh', scatter_dimension=0, tiled=True)]
  transfers between devices with their start and end apart: 2 -> 0, of which waited for: 1 -> 0; matrix products, arithmetic and copies ran while one was open for 0% -> 0% of each run, Pallas kernels for 0% -> 0%
where the time goes in v1:
time: 67 us; the launch traced here: 66.6 us
  Pallas kernels  59 us (88%)
  local copies, waits for them, and re-layouts  7.54 us (11%)
    pallas_call x1, Pallas kernels, body(): pl.pallas_call(kernel, out_shape=jax.ShapeDtypeStruct((16, 2, 80), F32),...  59 us
    unnamed x29, local copies, waits for them, and re-layouts  7.54 us

profile of v1, /device:TPU:1, one launch (start us, length us, event | category | flops | bytes accessed | tf_op | source)
XLA Modules:
  0.0 66.6 jit_solution(9267249108169054724)
XLA Ops:
  0.0 0.0 copy-start.7
  0.0 0.0 copy-start.13
  0.0 0.0 copy-start.9
  0.0 0.0 copy-start.11
  0.0 0.0 copy-start.12
  0.0 0.0 copy-start.8
  0.0 0.0 copy-start.10
  0.0 0.6 copy-done.7
  0.7 0.0 copy-done.13
  0.7 0.0 copy-done.9
  0.7 0.0 copy-done.11
  0.7 0.0 copy-done.12
  0.7 0.0 copy-done.8
  0.8 0.0 copy-done.10
  0.8 0.0 copy-start
  0.8 0.9 %copy-done = bf16[1024,80]{0,1:T(8,128)(2,1)S(1)} copy-done((bf16[1024,80]{0,1:T(8,128)(2,1)S(1)}, bf16[1024,80]{0,1:T(8,128)(2,1)}, u32[]{:S(2)}) %copy-start) | copy-done | bytes 163864
  1.7 0.0 copy-start.1
  1.7 0.9 %copy-done.1 = bf16[512,1,128]{2,0,1:T(8,128)(2,1)S(1)} copy-done((bf16[512,1,128]{2,0,1:T(8,128)(2,1)S(1)}, bf16[512,1,128]{2,0,1:T(8,128)(2,1)}, u32[]{:S(2)}) %copy-start.1) | copy-done | bytes 131096
  2.6 0.0 copy-start.2
  2.6 0.9 %copy-done.2 = bf16[512,1,128]{2,0,1:T(8,128)(2,1)S(1)} copy-done((bf16[512,1,128]{2,0,1:T(8,128)(2,1)S(1)}, bf16[512,1,128]{2,0,1:T(8,128)(2,1)}, u32[]{:S(2)}) %copy-start.2) | copy-done | bytes 131096
  3.5 0.0 copy-start.3
  3.5 0.9 %copy-done.3 = bf16[2,256,1,128]{3,1,2,0:T(8,128)(2,1)S(1)} copy-done((bf16[2,256,1,128]{3,1,2,0:T(8,128)(2,1)S(1)}, bf16[2,256,1,128]{3,1,2,0:T(8,128)(2,1)}, u32[]{:S(2)}) %copy-start.3) | copy-done | bytes 131096
  4.4 0.0 copy-start.4
  4.4 0.9 %copy-done.4 = bf16[2,256,1,128]{3,1,2,0:T(8,128)(2,1)S(1)} copy-done((bf16[2,256,1,128]{3,1,2,0:T(8,128)(2,1)S(1)}, bf16[2,256,1,128]{3,1,2,0:T(8,128)(2,1)}, u32[]{:S(2)}) %copy-start.4) | copy-done | bytes 131096
  5.3 0.0 copy-start.5
  5.3 0.8 %copy-done.5 = bf16[256,1,128]{2,0,1:T(8,128)(2,1)S(1)} copy-done((bf16[256,1,128]{2,0,1:T(8,128)(2,1)S(1)}, bf16[256,1,128]{2,0,1:T(8,128)(2,1)}, u32[]{:S(2)}) %copy-start.5) | copy-done | bytes 65560
  6.1 0.0 copy-start.6
  6.1 0.8 %copy-done.6 = bf16[256,1,128]{2,0,1:T(8,128)(2,1)S(1)} copy-done((bf16[256,1,128]{2,0,1:T(8,128)(2,1)S(1)}, bf16[256,1,128]{2,0,1:T(8,128)(2,1)}, u32[]{:S(2)}) %copy-start.6) | copy-done | bytes 65560
  7.0 59.0 %shard_map.136 = f32[16,2,80]{2,1,0:T(2,128)S(1)} custom-call(bf16[32,128]{1,0:T(8,128)(2,1)S(1)} %bitcast.18, bf16[256,128]{1,0:T(8,128)(2,1)S(1)} %bitcast.16, bf16[256,128]{1,0:T(8,128)(2,1)S(1)} %bitcast.17, bf16[512,128]{1,0:T(8,128)(2,1)S(1)} %bitcast.12, bf16[512,128]{1,0:T(8,128)(2,1)S(1)} %bitcast.13, bf16[2,256,128]{2,1,0:T(8,128)(2,1)S(1)} %bitcast.14, ...), custom_call_target="tpu_custom_call" | custom-call | tf_op jit(solution)/shard_map/pallas_call | solution.py:369
  66.0 0.6 copy.16
Async XLA Ops:
  0.0 0.7 %copy-start.7 = (bf16[2,2,8,128]{3,2,1,0:T(8,128)(2,1)S(1)}, bf16[2,2,8,128]{3,2,1,0:T(8,128)(2,1)}, u32[]{:S(2)}) copy-start(bf16[2,2,8,128]{3,2,1,0:T(8,128)(2,1)} %param.14) | copy-start | bytes 24580
  0.0 0.7 %copy-start.13 = (s32[2]{0:T(128)S(1)}, s32[2]{0:T(128)}, u32[]{:S(2)}) copy-start(s32[2]{0:T(128)} %cont_len_ref.1) | copy-start | bytes 28
  0.0 0.7 %copy-start.9 = (bf16[2,2,1,128]{3,1,2,0:T(2,128)(2,1)S(1)}, bf16[2,2,1,128]{3,1,2,0:T(2,128)(2,1)}, u32[]{:S(2)}) copy-start(bf16[2,2,1,128]{3,1,2,0:T(2,128)(2,1)} %param.16) | copy-start | bytes 3076
  0.0 0.7 %copy-start.11 = (s32[16]{0:T(128)S(1)}, s32[16]{0:T(128)}, u32[]{:S(2)}) copy-start(s32[16]{0:T(128)} %group_prompt_ref.1) | copy-start | bytes 196
  0.0 0.7 %copy-start.12 = (s32[16]{0:T(128)S(1)}, s32[16]{0:T(128)}, u32[]{:S(2)}) copy-start(s32[16]{0:T(128)} %prompt_len_ref.1) | copy-start | bytes 196
  0.0 0.7 %copy-start.8 = (bf16[2,2,1,128]{3,1,2,0:T(2,128)(2,1)S(1)}, bf16[2,2,1,128]{3,1,2,0:T(2,128)(2,1)}, u32[]{:S(2)}) copy-start(bf16[2,2,1,128]{3,1,2,0:T(2,128)(2,1)} %param.15) | copy-start | bytes 3076
  0.0 0.7 %copy-start.10 = (s32[128]{0:T(128)S(1)}, s32[128]{0:T(128)}, u32[]{:S(2)}) copy-start(s32[128]{0:T(128)} %param.25) | copy-start | bytes 1540
  0.8 0.9 %copy-start = (bf16[1024,80]{0,1:T(8,128)(2,1)S(1)}, bf16[1024,80]{0,1:T(8,128)(2,1)}, u32[]{:S(2)}) copy-start(bf16[1024,80]{0,1:T(8,128)(2,1)} %param.27) | copy-start | bytes 491524
  1.7 0.9 %copy-start.1 = (bf16[512,1,128]{2,0,1:T(8,128)(2,1)S(1)}, bf16[512,1,128]{2,0,1:T(8,128)(2,1)}, u32[]{:S(2)}) copy-start(bf16[512,1,128]{2,0,1:T(8,128)(2,1)} %param.19) | copy-start | bytes 393220
  2.6 0.9 %copy-start.2 = (bf16[512,1,128]{2,0,1:T(8,128)(2,1)S(1)}, bf16[512,1,128]{2,0,1:T(8,128)(2,1)}, u32[]{:S(2)}) copy-start(bf16[512,1,128]{2,0,1:T(8,128)(2,1)} %param.20) | copy-start | bytes 393220
  3.5 0.9 %copy-start.3 = (bf16[2,256,1,128]{3,1,2,0:T(8,128)(2,1)S(1)}, bf16[2,256,1,128]{3,1,2,0:T(8,128)(2,1)}, u32[]{:S(2)}) copy-start(bf16[2,256,1,128]{3,1,2,0:T(8,128)(2,1)} %param.21) | copy-start | bytes 393220
  4.4 0.9 %copy-start.4 = (bf16[2,256,1,128]{3,1,2,0:T(8,128)(2,1)S(1)}, bf16[2,256,1,128]{3,1,2,0:T(8,128)(2,1)}, u32[]{:S(2)}) copy-start(bf16[2,256,1,128]{3,1,2,0:T(8,128)(2,1)} %param.22) | copy-start | bytes 393220
  5.3 0.8 %copy-start.5 = (bf16[256,1,128]{2,0,1:T(8,128)(2,1)S(1)}, bf16[256,1,128]{2,0,1:T(8,128)(2,1)}, u32[]{:S(2)}) copy-start(bf16[256,1,128]{2,0,1:T(8,128)(2,1)} %param.17) | copy-start | bytes 196612
  6.1 0.8 %copy-start.6 = (bf16[256,1,128]{2,0,1:T(8,128)(2,1)S(1)}, bf16[256,1,128]{2,0,1:T(8,128)(2,1)}, u32[]{:S(2)}) copy-start(bf16[256,1,128]{2,0,1:T(8,128)(2,1)} %param.18) | copy-start | bytes 196612

commit v2 on v1

--- a/solution.py
+++ b/solution.py
@@ -53,6 +53,30 @@
 def with_ones(values):
     flipped = jnp.transpose(values.astype(F32))
     return jnp.concatenate([flipped, jnp.ones((16, values.shape[0]), F32)], axis=0).astype(BF16)
+
+
+def swing(i, middle):
+    return middle + (i + 1) // 2 * (1 - 2 * (i % 2))
+
+
+def attend(keys, flipped, rows, visible=None):
+    scores = dot_nt(keys, rows) * SCALING
+    if visible is not None:
+        scores = jnp.where(visible, scores, NEG)
+    peak = jnp.max(scores, axis=0, keepdims=True)
+    weights = jnp.exp(scores - peak).astype(BF16)
+    return peak, dot(flipped, weights)[0:136]
+
+
+def join(peaks, parts):
+    top = functools.reduce(jnp.maximum, peaks)
+    total = None
+    for peak, part in zip(peaks, parts):
+        term = jnp.exp(peak - top) * part
+        total = term if total is None else total + term
+    width = top.shape[1]
+    stats = jnp.where(iota((8, width), 0) == 1, top, total[128:136])
+    return total[0:128], stats
 
 
 def kernel(
@@ -72,17 +96,16 @@
     cont_len_ref,
     out_ref,
     q_all,
-    pk,
-    pv,
+    kv,
     sk,
     sv,
     ck,
     cv,
     wt,
-    pvt,
-    svt,
-    member,
-    x_send,
+    places,
+    pick,
+    spread,
+    parts,
     x_recv,
     z_send,
     z_recv,
@@ -94,6 +117,10 @@
     own_sem,
     swap_ss,
     swap_rs,
+    kv_ss,
+    kv_rs,
+    fw_ss,
+    fw_rs,
     q_ss,
     q_rs,
     x_ss,
@@ -138,8 +165,8 @@
                 (q_in, q_all.at[chip]),
                 (ck_in, ck),
                 (cv_in, cv),
-                (pk_in, pk.at[c]),
-                (pv_in, pv.at[c]),
+                (pk_in, kv.at[x, c, 0]),
+                (pv_in, kv.at[x, c, 1]),
                 (sk_in, sk.at[c]),
                 (sv_in, sv.at[c]),
                 (w_in, wt.at[c, pl.ds(0, 80)]),
@@ -149,9 +176,31 @@
     for copy in local:
         copy.start()
     wt[:, 80:, :] = jnp.zeros((2, 48, wt.shape[2]), BF16)
+
+    cont_prompt = cont_prompt_ref[...]
+    conts = iota((1, 128), 1)
+    on_core = (conts // 2) % 2 == c
+    members = [
+        jnp.where((cont_prompt == group_prompt_ref[(g * NZ + z) // 2]) & on_core, 1.0, 0.0)
+        for g in range(NX)
+    ]
+    members = jnp.concatenate(members + [jnp.zeros((4, 128), F32)], axis=0)
+    before = jnp.where(iota((128, 128), 0) < iota((128, 128), 1), 1.0, 0.0).astype(BF16)
+    ranks = ((dot(members.astype(BF16), before) + 1.0) * members).astype(BF16)
+    lane = iota((128, 256), 1)
+    inside = (lane % 16).astype(F32)[0:8]
+    for g in range(NX):
+        cont = (g * NZ + lane // ROWS) * 4 + c * 2 + (lane % ROWS) // 16
+        widen = jnp.where(iota((128, 256), 0) == cont, 1.0, 0.0).astype(BF16)
+        ranked = dot(ranks, widen)
+        places[g] = jnp.where(ranked > 0.5, ranked * 16.0 - 16.0 + inside, -1.0)
+    place_row = iota((128, 256), 0).astype(F32)
+    for g in range(NX):
+        pick[g] = jnp.where(place_row == places[g, pl.ds(x, 1)], 1.0, 0.0).astype(BF16)
+        spread[g] = jnp.where(place_row == places[x, pl.ds(g, 1)], 1.0, 0.0).astype(BF16)
+
     for copy in local[:3]:
         copy.wait()
-
     q_own = q_all[chip]
     first = iota((ROWS, 1), 0) < 16
     past0 = dot_nt(q_own, ck[0]) * SCALING
@@ -172,125 +221,114 @@
         fresh_w.astype(F32), axis=1, keepdims=True
     )
     own_part = jnp.where(first, dot(past_w, cv[0]), dot(past_w, cv[1])) + dot(fresh_w, nv)
-
-    prompt = group_prompt_ref[chip // 2]
-    length = prompt_len_ref[prompt]
-    prompts = jnp.broadcast_to(cont_prompt_ref[...].astype(F32), (8, 128)).astype(BF16)
-    for g in range(NX):
-        lane = iota((128, 256), 1)
-        cont = (g * NZ + lane // ROWS) * 4 + c * 2 + (lane % ROWS) // 16
-        spread = jnp.where(iota((128, 256), 0) == cont, 1.0, 0.0).astype(BF16)
-        prompt_of = dot(prompts, spread)
-        member[g] = jnp.where(prompt_of == jnp.full((8, 256), prompt, jnp.int32).astype(F32), 1.0, 0.0)
+    for copy in local[3:]:
+        copy.wait()
 
     pl.semaphore_wait(barrier, CHIPS - 1 + 15)
 
-    def q_copy(k):
+    def chip_at(n):
+        return lax.rem(x + n // NZ, NX) * NZ + lax.rem(z + n % NZ, NZ)
+
+    def far_first(n):
+        return swing(n // NZ, 2) * NZ + swing(n % NZ, 4)
+
+    def q_copy(n):
         block = q_all.at[chip]
-        return remote(block, block, q_ss.at[k], q_rs.at[k], lax.rem(chip + k, CHIPS), y, c)
-
-    loop(1, CHIPS, lambda k: q_copy(k).start())
+        return remote(block, block, q_ss.at[n], q_rs.at[n], chip_at(n), y, c)
+
+    loop(0, CHIPS - 1, lambda n: q_copy(far_first(n)).start())
+
+    def kv_copy(k):
+        block = kv.at[x, c]
+        return remote(block, block, kv_ss.at[k], kv_rs.at[k], lax.rem(x + k, NX) * NZ + z, y, c)
+
+    def fw_copy(k):
+        block = kv.at[lax.rem(x + NX - k, NX), c]
+        return remote(block, block, fw_ss.at[k], fw_rs.at[k], chip, y, other)
+
     swaps = [
-        remote(src, dst, swap_ss.at[n], swap_rs.at[n], chip, y, other)
-        for n, (src, dst) in enumerate(
-            [
-                (pk_in, pk.at[c]),
-                (pv_in, pv.at[c]),
-                (sk_in, sk.at[c]),
-                (sv_in, sv.at[c]),
-                (w_in, wt.at[c, pl.ds(0, 80)]),
-            ]
-        )
+        remote(src, src, swap_ss.at[n], swap_rs.at[n], chip, y, other)
+        for n, src in enumerate([sk.at[c], sv.at[c], wt.at[c, pl.ds(0, 80)]])
     ]
+    for k in (2, 1, 3):
+        kv_copy(k).start()
+    fw_copy(0).start()
     for copy in swaps:
         copy.start()
-    for copy in local[3:]:
-        copy.wait()
-    pvt[c] = with_ones(pv[c])
-    svt[c] = with_ones(sv[c])
+    for k in (1, 3, 2):
+        kv_copy(k).wait_recv()
+        fw_copy(k).start()
+
+    def rows_of(g):
+        return q_all[pl.ds(g * NZ, NZ)].reshape(NZ * ROWS, HD)
+
+    def prefix_block(n):
+        block = kv.at[lax.rem(x + NX - n // 2, NX), lax.rem(c + n, 2)]
+        peak, part = attend(block[0], with_ones(block[1]), rows_of(x))
+        parts[n, 0:128] = part[0:128]
+        parts[n, 128:136] = jnp.where(iota((8, 256), 0) == 1, peak, part[128:136])
+
+    loop(1, NZ, lambda n: q_copy(n).wait_recv())
+    fw_copy(0).wait_recv()
+    loop(0, 2, prefix_block)
+
     for copy in swaps:
         copy.wait_recv()
-    pvt[other] = with_ones(pv[other])
-    svt[other] = with_ones(sv[other])
-
-    def group_partial(g, put):
-        rows = q_all[pl.ds(g * NZ, NZ)].reshape(NZ * ROWS, HD)
-        mine = member[g][0:1] > 0.5
-        peaks, parts = [], []
-        for b in range(2):
-            scores = dot_nt(pk[b], rows) * SCALING
-            peak = jnp.max(scores, axis=0, keepdims=True)
-            weights = jnp.exp(scores - peak).astype(BF16)
-            peaks.append(peak)
-            parts.append(dot(pvt[b], weights))
-        for b in range(2):
-            scores = dot_nt(sk[b], rows) * SCALING
-            place = ((z % 2) * 2 + b) * 512 + iota((512, 1), 0)
-            scores = jnp.where(place < length, scores, NEG)
-            peak = jnp.max(scores, axis=0, keepdims=True)
-            weights = jnp.exp(scores - peak).astype(BF16)
-            peaks.append(jnp.where(mine, peak, NEG))
-            parts.append(dot(svt[b], weights))
-        put(*join(peaks, parts))
-
-    def join(peaks, parts):
-        top = functools.reduce(jnp.maximum, peaks)
-        total = None
-        for peak, part in zip(peaks, parts):
-            term = jnp.exp(peak - top) * part[0:136]
-            total = term if total is None else total + term
-        stats = jnp.where(iota((8, 256), 0) == 1, top, total[128:136])
-        return total[0:128], stats
+    length = prompt_len_ref[group_prompt_ref[chip // 2]]
+    flipped = [with_ones(sv[b]) for b in range(2)]
+    loop(NZ, CHIPS, lambda n: q_copy(n).wait_recv())
+    picked = functools.reduce(jnp.add, [dot(pick[g], rows_of(g)) for g in range(NX)]).astype(BF16)
+    pairs = [
+        attend(
+            sk[b],
+            flipped[b],
+            picked,
+            ((z % 2) * 2 + b) * 512 + iota((512, 1), 0) < length,
+        )
+        for b in range(2)
+    ]
+    part, stats = join([p[0] for p in pairs], [p[1] for p in pairs])
+    x_recv[x, 0:128] = part
+    x_recv[x, 128:136] = stats
 
     def x_copy(k):
-        to = lax.rem(x + k, NX)
-        return remote(x_send.at[to], x_recv.at[x], x_ss.at[k], x_rs.at[k], to * NZ + z, y, c)
-
-    def q_wait(g):
-        def one(n):
-            k = lax.rem(chip - (g * NZ + n) + CHIPS, CHIPS)
-
-            @pl.when(k > 0)
-            def _():
-                q_copy(k).wait_recv()
-
-        loop(0, NZ, one)
-
-    def group_step(k):
-        g = lax.rem(x + k, NX)
-        q_wait(g)
-
-        def put_send(part, stats):
-            x_send[g, 0:128] = part
-            x_send[g, 128:136] = stats
-
-        group_partial(g, put_send)
+        block = x_recv.at[x]
+        return remote(block, block, x_ss.at[k], x_rs.at[k], lax.rem(x + k, NX) * NZ + z, y, c)
+
+    for k in (2, 1, 3):
         x_copy(k).start()
 
-    loop(1, NX, group_step)
-    q_wait(x)
-
-    def put_own(part, stats):
-        x_recv[x, 0:128] = part
-        x_recv[x, 128:136] = stats
-
-    group_partial(x, put_own)
-    loop(1, NX, lambda k: x_copy(k).wait_recv())
-
-    part, stats = join([x_recv[s, 129:130] for s in range(NX)], [x_recv[s] for s in range(NX)])
+    for k in range(1, NX):
+        fw_copy(k).wait_recv()
+    loop(2, 8, prefix_block)
+    part, stats = join([parts[n, 129:130] for n in range(8)], [parts[n] for n in range(8)])
+    for k in range(1, NX):
+        x_copy(k).wait_recv()
+    peaks, sums = [stats[1:2]], [jnp.concatenate([part, stats], axis=0)]
+    for g in range(NX):
+        compact = x_recv[g]
+        high = compact.astype(BF16)
+        rest = compact - high.astype(F32)
+        middle = rest.astype(BF16)
+        low = (rest - middle.astype(F32)).astype(BF16)
+        wide = dot(high, spread[g]) + dot(middle, spread[g]) + dot(low, spread[g])
+        peaks.append(jnp.where(places[x, pl.ds(g, 1)] >= 0.0, wide[129:130], NEG))
+        sums.append(wide)
+    part, stats = join(peaks, sums)
+
     by_row = jnp.transpose(part)
     for t in range(NZ):
         half = stats[:, (t // 4) * 128 : (t // 4 + 1) * 128]
         turned = half if t % 4 == 0 else pltpu.roll(half, 128 - (t % 4) * ROWS, 1)
         z_send[t, 0:ROWS] = by_row[t * ROWS : (t + 1) * ROWS]
         z_send[t, ROWS : ROWS + 8] = turned
-    z_recv[z] = z_send[z]
 
     def z_copy(k):
         to = lax.rem(z + k, NZ)
         return remote(z_send.at[to], z_recv.at[z], z_ss.at[k], z_rs.at[k], x * NZ + to, y, c)
 
-    loop(1, NZ, lambda k: z_copy(k).start())
+    loop(0, NZ - 1, lambda n: z_copy(swing(n, 4)).start())
+    z_recv[z] = z_send[z]
     loop(1, NZ, lambda k: z_copy(k).wait_recv())
 
     side = jnp.concatenate(
@@ -309,12 +347,12 @@
         weighted = weighted + factor * z_recv[s, 0:ROWS]
     att[chip] = (weighted / total).astype(BF16)
 
-    def a_copy(k):
+    def a_copy(n):
         block = att.at[chip]
-        return remote(block, block, a_ss.at[k], a_rs.at[k], lax.rem(chip + k, CHIPS), y, c)
-
-    loop(1, CHIPS, lambda k: a_copy(k).start())
-    loop(1, CHIPS, lambda k: a_copy(k).wait_recv())
+        return remote(block, block, a_ss.at[n], a_rs.at[n], chip_at(n), y, c)
+
+    loop(0, CHIPS - 1, lambda n: a_copy(far_first(n)).start())
+    loop(1, CHIPS, lambda n: a_copy(n).wait_recv())
 
     att_f32[...] = att[...].reshape(CHIPS * ROWS, HD).astype(F32)
     for h in range(GROUP):
@@ -323,14 +361,14 @@
         y_send[b] = dot_nt(flat[...], wt[b]).reshape(NY, 16, 128)
     y_recv[yc] = y_send[c, y]
 
-    def y_copy(k):
-        to = lax.rem(yc + k, 16)
+    def y_copy(n):
+        to_y, to_c = lax.rem(y + n // 2, NY), lax.rem(c + n, 2)
         return remote(
-            y_send.at[to % 2, to // 2], y_recv.at[yc], y_ss.at[k], y_rs.at[k], chip, to // 2, to % 2
+            y_send.at[to_c, to_y], y_recv.at[yc], y_ss.at[n], y_rs.at[n], chip, to_y, to_c
         )
 
-    loop(1, 16, lambda k: y_copy(k).start())
-    loop(1, 16, lambda k: y_copy(k).wait_recv())
+    loop(0, 15, lambda n: y_copy(swing(n // 2, 4) * 2 + 1 - n % 2).start())
+    loop(1, 16, lambda n: y_copy(n).wait_recv())
     for b in range(2):
         summed = functools.reduce(jnp.add, [y_recv[n * 2 + b] for n in range(NY)])
         for n in range(4):
@@ -339,11 +377,15 @@
 
     for copy in swaps:
         copy.wait_send()
-    loop(1, CHIPS, lambda k: q_copy(k).wait_send())
-    loop(1, NX, lambda k: x_copy(k).wait_send())
+    for k in range(NX):
+        fw_copy(k).wait_send()
+    for k in range(1, NX):
+        kv_copy(k).wait_send()
+        x_copy(k).wait_send()
+    loop(1, CHIPS, lambda n: q_copy(n).wait_send())
     loop(1, NZ, lambda k: z_copy(k).wait_send())
-    loop(1, CHIPS, lambda k: a_copy(k).wait_send())
-    loop(1, 16, lambda k: y_copy(k).wait_send())
+    loop(1, CHIPS, lambda n: a_copy(n).wait_send())
+    loop(1, 16, lambda n: y_copy(n).wait_send())
 
 
 def body(
@@ -373,18 +415,17 @@
         out_specs=vmem,
         scratch_shapes=[
             pltpu.VMEM((CHIPS, ROWS, HD), BF16),
-            pltpu.VMEM((2, 256, HD), BF16),
-            pltpu.VMEM((2, 256, HD), BF16),
+            pltpu.VMEM((NX, 2, 2, 256, HD), BF16),
             pltpu.VMEM((2, 512, HD), BF16),
             pltpu.VMEM((2, 512, HD), BF16),
             pltpu.VMEM((2, 256, HD), BF16),
             pltpu.VMEM((2, 256, HD), BF16),
             pltpu.VMEM((2, 128, 1024), BF16),
-            pltpu.VMEM((2, 144, 256), BF16),
-            pltpu.VMEM((2, 144, 512), BF16),
             pltpu.VMEM((NX, 8, 256), F32),
-            pltpu.VMEM((NX, 136, 256), F32),
-            pltpu.VMEM((NX, 136, 256), F32),
+            pltpu.VMEM((NX, 128, 256), BF16),
+            pltpu.VMEM((NX, 128, 256), BF16),
+            pltpu.VMEM((8, 136, 256), F32),
+            pltpu.VMEM((NX, 136, 128), F32),
             pltpu.VMEM((NZ, 40, 128), F32),
             pltpu.VMEM((NZ, 40, 128), F32),
             pltpu.VMEM((CHIPS, ROWS, HD), BF16),
@@ -393,8 +434,12 @@
             pltpu.VMEM((2, NY, 16, 128), F32),
             pltpu.VMEM((16, 16, 128), F32),
             dma((8,)),
-            dma((5,)),
-            dma((5,)),
+            dma((3,)),
+            dma((3,)),
+            dma((NX,)),
+            dma((NX,)),
+            dma((NX,)),
+            dma((NX,)),
             dma((CHIPS,)),
             dma((CHIPS,)),
             dma((NX,)),
@@ -407,7 +452,7 @@
             dma((16,)),
         ],
         compiler_params=pltpu.CompilerParams(
-            collective_id=0, has_side_effects=True, vmem_limit_bytes=32 << 20
+            collective_id=0, has_side_effects=True, vmem_limit_bytes=60 << 20
         ),
     )(
         queries.reshape(ROWS, HD),

time: 67 us -> 60.9 us (0.909)
  local copies, waits for them, and re-layouts: 7.54 us -> 1.32 us
    unnamed x29 -> x1, local copies, waits for them, and re-layouts: 7.54 us -> 1.32 us
where the time goes in v2:
time: 60.9 us; the launch traced here: 60.6 us
  Pallas kernels  59.3 us (97%)
  local copies, waits for them, and re-layouts  1.32 us (2%)
    pallas_call x1, Pallas kernels, body(): pl.pallas_call(kernel, out_shape=jax.ShapeDtypeStruct((16, 2, 80), F32),...  59.3 us
    unnamed x1, local copies, waits for them, and re-layouts  1.32 us

profile of v2, /device:TPU:1, one launch (start us, length us, event | category | flops | bytes accessed | tf_op | source)
XLA Modules:
  0.0 60.6 jit_solution(7947136910915948751)
XLA Ops:
  0.0 59.3 %shard_map.136 = f32[16,2,80]{2,1,0:T(2,128)} custom-call(bf16[32,128]{1,0:T(8,128)(2,1)} %bitcast.18, bf16[256,128]{1,0:T(8,128)(2,1)} %bitcast.16, bf16[256,128]{1,0:T(8,128)(2,1)} %bitcast.17, bf16[512,128]{1,0:T(8,128)(2,1)} %bitcast.12, bf16[512,128]{1,0:T(8,128)(2,1)} %bitcast.13, bf16[2,256,128]{2,1,0:T(8,128)(2,1)} %bitcast.14, ...), custom_call_target="tpu_custom_call" | custom-call | tf_op jit(solution)/shard_map/pallas_call | solution.py:411
  59.3 1.3 %copy.16 = f32[16,2,80]{2,1,0:T(2,128)} copy(f32[16,2,80]{2,1,0:T(2,128)} %shard_map.136) | data formatting | bytes 20480

commit v3 on v2

--- a/solution.py
+++ b/solution.py
@@ -55,8 +55,8 @@
     return jnp.concatenate([flipped, jnp.ones((16, values.shape[0]), F32)], axis=0).astype(BF16)
 
 
-def swing(i, middle):
-    return middle + (i + 1) // 2 * (1 - 2 * (i % 2))
+X_STEPS, Z_STEPS, Y_STEPS = (2, 1, 3, 0), (4, 3, 5, 2, 6, 1, 7, 0), (4, 3, 5, 2, 6, 1, 7, 0)
+FAR_FIRST = [(dx, dz) for dx in X_STEPS for dz in Z_STEPS if dx or dz]
 
 
 def attend(keys, flipped, rows, visible=None):
@@ -141,22 +141,21 @@
 
     barrier = pltpu.get_barrier_semaphore()
 
-    def greet_plane(k):
+    x_to = [lax.rem(x + d, NX) * NZ for d in range(NX)]
+    z_to = [lax.rem(z + d, NZ) for d in range(NZ)]
+    y_to = [lax.rem(y + d, NY) for d in range(NY)]
+
+    def greet(to_chip, to_y, to_c):
         pl.semaphore_signal(
-            barrier,
-            inc=1,
-            device_id={"seq": lax.rem(chip + k, CHIPS) * 2 + c, "kvh": y},
-            device_id_type=MESH,
+            barrier, inc=1, device_id={"seq": to_chip * 2 + to_c, "kvh": to_y}, device_id_type=MESH
         )
 
-    def greet_column(k):
-        to = lax.rem(yc + k, 16)
-        pl.semaphore_signal(
-            barrier, inc=1, device_id={"seq": chip * 2 + to % 2, "kvh": to // 2}, device_id_type=MESH
-        )
-
-    loop(1, CHIPS, greet_plane)
-    loop(1, 16, greet_column)
+    for dx, dz in FAR_FIRST:
+        greet(x_to[dx] + z_to[dz], y, c)
+    for dy in Y_STEPS:
+        greet(chip, y_to[dy], other)
+        if dy:
+            greet(chip, y_to[dy], c)
 
     local = [
         pltpu.make_async_copy(src, dst, own_sem.at[n])
@@ -176,6 +175,36 @@
     for copy in local:
         copy.start()
     wt[:, 80:, :] = jnp.zeros((2, 48, wt.shape[2]), BF16)
+
+    for copy in local:
+        copy.wait()
+
+    pl.semaphore_wait(barrier, CHIPS - 1 + 15)
+
+    def q_copy(dx, dz):
+        block = q_all.at[chip]
+        return remote(block, block, q_ss, q_rs.at[1 if dx else 0], x_to[dx] + z_to[dz], y, c)
+
+    for dx, dz in FAR_FIRST:
+        q_copy(dx, dz).start()
+
+    def kv_copy(k):
+        block = kv.at[x, c]
+        return remote(block, block, kv_ss.at[k], kv_rs.at[k], x_to[k] + z, y, c)
+
+    def fw_copy(k):
+        block = kv.at[lax.rem(x + NX - k, NX), c]
+        return remote(block, block, fw_ss.at[k], fw_rs.at[k], chip, y, other)
+
+    swaps = [
+        remote(src, src, swap_ss.at[n], swap_rs.at[n], chip, y, other)
+        for n, src in enumerate([sk.at[c], sv.at[c], wt.at[c, pl.ds(0, 80)]])
+    ]
+    for k in (2, 1, 3):
+        kv_copy(k).start()
+    fw_copy(0).start()
+    for copy in swaps:
+        copy.start()
 
     cont_prompt = cont_prompt_ref[...]
     conts = iota((1, 128), 1)
@@ -199,8 +228,6 @@
         pick[g] = jnp.where(place_row == places[g, pl.ds(x, 1)], 1.0, 0.0).astype(BF16)
         spread[g] = jnp.where(place_row == places[x, pl.ds(g, 1)], 1.0, 0.0).astype(BF16)
 
-    for copy in local[:3]:
-        copy.wait()
     q_own = q_all[chip]
     first = iota((ROWS, 1), 0) < 16
     past0 = dot_nt(q_own, ck[0]) * SCALING
@@ -221,40 +248,12 @@
         fresh_w.astype(F32), axis=1, keepdims=True
     )
     own_part = jnp.where(first, dot(past_w, cv[0]), dot(past_w, cv[1])) + dot(fresh_w, nv)
-    for copy in local[3:]:
-        copy.wait()
-
-    pl.semaphore_wait(barrier, CHIPS - 1 + 15)
-
-    def chip_at(n):
-        return lax.rem(x + n // NZ, NX) * NZ + lax.rem(z + n % NZ, NZ)
-
-    def far_first(n):
-        return swing(n // NZ, 2) * NZ + swing(n % NZ, 4)
-
-    def q_copy(n):
-        block = q_all.at[chip]
-        return remote(block, block, q_ss.at[n], q_rs.at[n], chip_at(n), y, c)
-
-    loop(0, CHIPS - 1, lambda n: q_copy(far_first(n)).start())
-
-    def kv_copy(k):
-        block = kv.at[x, c]
-        return remote(block, block, kv_ss.at[k], kv_rs.at[k], lax.rem(x + k, NX) * NZ + z, y, c)
-
-    def fw_copy(k):
-        block = kv.at[lax.rem(x + NX - k, NX), c]
-        return remote(block, block, fw_ss.at[k], fw_rs.at[k], chip, y, other)
-
-    swaps = [
-        remote(src, src, swap_ss.at[n], swap_rs.at[n], chip, y, other)
-        for n, src in enumerate([sk.at[c], sv.at[c], wt.at[c, pl.ds(0, 80)]])
-    ]
-    for k in (2, 1, 3):
-        kv_copy(k).start()
-    fw_copy(0).start()
-    for copy in swaps:
-        copy.start()
+    def arrived(ref, sem):
+        remote(ref, ref, q_ss, sem, chip, y, other).wait_recv()
+
+    def left(ref, sem):
+        remote(ref, ref, sem, q_rs.at[0], chip, y, other).wait_send()
+
     for k in (1, 3, 2):
         kv_copy(k).wait_recv()
         fw_copy(k).start()
@@ -268,7 +267,7 @@
         parts[n, 0:128] = part[0:128]
         parts[n, 128:136] = jnp.where(iota((8, 256), 0) == 1, peak, part[128:136])
 
-    loop(1, NZ, lambda n: q_copy(n).wait_recv())
+    arrived(q_all.at[pl.ds(0, NZ - 1)], q_rs.at[0])
     fw_copy(0).wait_recv()
     loop(0, 2, prefix_block)
 
@@ -276,7 +275,7 @@
         copy.wait_recv()
     length = prompt_len_ref[group_prompt_ref[chip // 2]]
     flipped = [with_ones(sv[b]) for b in range(2)]
-    loop(NZ, CHIPS, lambda n: q_copy(n).wait_recv())
+    arrived(q_all.at[pl.ds(0, CHIPS - NZ)], q_rs.at[1])
     picked = functools.reduce(jnp.add, [dot(pick[g], rows_of(g)) for g in range(NX)]).astype(BF16)
     pairs = [
         attend(
@@ -293,7 +292,7 @@
 
     def x_copy(k):
         block = x_recv.at[x]
-        return remote(block, block, x_ss.at[k], x_rs.at[k], lax.rem(x + k, NX) * NZ + z, y, c)
+        return remote(block, block, x_ss.at[k], x_rs.at[k], x_to[k] + z, y, c)
 
     for k in (2, 1, 3):
         x_copy(k).start()
@@ -302,6 +301,13 @@
         fw_copy(k).wait_recv()
     loop(2, 8, prefix_block)
     part, stats = join([parts[n, 129:130] for n in range(8)], [parts[n] for n in range(8)])
+    left(q_all.at[pl.ds(0, CHIPS - 1)], q_ss)
+    for copy in swaps:
+        copy.wait_send()
+    for k in range(NX):
+        fw_copy(k).wait_send()
+    for k in range(1, NX):
+        kv_copy(k).wait_send()
     for k in range(1, NX):
         x_copy(k).wait_recv()
     peaks, sums = [stats[1:2]], [jnp.concatenate([part, stats], axis=0)]
@@ -323,13 +329,13 @@
         z_send[t, 0:ROWS] = by_row[t * ROWS : (t + 1) * ROWS]
         z_send[t, ROWS : ROWS + 8] = turned
 
-    def z_copy(k):
-        to = lax.rem(z + k, NZ)
-        return remote(z_send.at[to], z_recv.at[z], z_ss.at[k], z_rs.at[k], x * NZ + to, y, c)
-
-    loop(0, NZ - 1, lambda n: z_copy(swing(n, 4)).start())
+    for dz in Z_STEPS[:-1]:
+        to = z_to[dz]
+        remote(z_send.at[to], z_recv.at[z], z_ss, z_rs, x_to[0] + to, y, c).start()
     z_recv[z] = z_send[z]
-    loop(1, NZ, lambda k: z_copy(k).wait_recv())
+    for k in range(1, NX):
+        x_copy(k).wait_send()
+    arrived(z_recv.at[pl.ds(0, NZ - 1)], z_rs)
 
     side = jnp.concatenate(
         [z_recv[s, ROWS + 1 : ROWS + 2] for s in range(NZ)]
@@ -347,45 +353,32 @@
         weighted = weighted + factor * z_recv[s, 0:ROWS]
     att[chip] = (weighted / total).astype(BF16)
 
-    def a_copy(n):
+    for dx, dz in FAR_FIRST:
         block = att.at[chip]
-        return remote(block, block, a_ss.at[n], a_rs.at[n], chip_at(n), y, c)
-
-    loop(0, CHIPS - 1, lambda n: a_copy(far_first(n)).start())
-    loop(1, CHIPS, lambda n: a_copy(n).wait_recv())
+        remote(block, block, a_ss, a_rs, x_to[dx] + z_to[dz], y, c).start()
+    left(z_send.at[pl.ds(0, NZ - 1)], z_ss)
+    arrived(att.at[pl.ds(0, CHIPS - 1)], a_rs)
 
     att_f32[...] = att[...].reshape(CHIPS * ROWS, HD).astype(F32)
     for h in range(GROUP):
         flat[:, h * HD : (h + 1) * HD] = att_f32[pl.ds(h, 128, stride=GROUP), :].astype(BF16)
     for b in range(2):
         y_send[b] = dot_nt(flat[...], wt[b]).reshape(NY, 16, 128)
+    for dy in Y_STEPS:
+        for dc in (1, 0):
+            if dy or dc:
+                to_y, to_c = y_to[dy], other if dc else c
+                remote(y_send.at[to_c, to_y], y_recv.at[yc], y_ss, y_rs, chip, to_y, to_c).start()
     y_recv[yc] = y_send[c, y]
-
-    def y_copy(n):
-        to_y, to_c = lax.rem(y + n // 2, NY), lax.rem(c + n, 2)
-        return remote(
-            y_send.at[to_c, to_y], y_recv.at[yc], y_ss.at[n], y_rs.at[n], chip, to_y, to_c
-        )
-
-    loop(0, 15, lambda n: y_copy(swing(n // 2, 4) * 2 + 1 - n % 2).start())
-    loop(1, 16, lambda n: y_copy(n).wait_recv())
+    left(att.at[pl.ds(0, CHIPS - 1)], a_ss)
+    arrived(y_recv.at[pl.ds(0, 15)], y_rs)
     for b in range(2):
         summed = functools.reduce(jnp.add, [y_recv[n * 2 + b] for n in range(NY)])
         for n in range(4):
             for i in range(2):
                 out_ref[n * 4 + b * 2 + i] = summed[n * 4 + i * 2 : n * 4 + i * 2 + 2, 0:80]
 
-    for copy in swaps:
-        copy.wait_send()
-    for k in range(NX):
-        fw_copy(k).wait_send()
-    for k in range(1, NX):
-        kv_copy(k).wait_send()
-        x_copy(k).wait_send()
-    loop(1, CHIPS, lambda n: q_copy(n).wait_send())
-    loop(1, NZ, lambda k: z_copy(k).wait_send())
-    loop(1, CHIPS, lambda n: a_copy(n).wait_send())
-    loop(1, 16, lambda n: y_copy(n).wait_send())
+    left(y_recv.at[pl.ds(0, 15)], y_ss)
 
 
 def body(
@@ -440,19 +433,19 @@
             dma((NX,)),
             dma((NX,)),
             dma((NX,)),
-            dma((CHIPS,)),
-            dma((CHIPS,)),
-            dma((NX,)),
-            dma((NX,)),
-            dma((NZ,)),
-            dma((NZ,)),
-            dma((CHIPS,)),
-            dma((CHIPS,)),
-            dma((16,)),
-            dma((16,)),
+            dma,
+            dma((2,)),
+            dma((NX,)),
+            dma((NX,)),
+            dma,
+            dma,
+            dma,
+            dma,
+            dma,
+            dma,
         ],
         compiler_params=pltpu.CompilerParams(
-            collective_id=0, has_side_effects=True, vmem_limit_bytes=60 << 20
+            collective_id=0, has_side_effects=True, vmem_limit_bytes=55168 << 10
         ),
     )(
         queries.reshape(ROWS, HD),

time: 60.9 us -> 56.7 us (0.931)
  Pallas kernels: 59.3 us -> 55.1 us
    pallas_call x1, Pallas kernels: 59.3 us -> 55.1 us  [body(): pl.pallas_call(kernel, out_shape=jax.ShapeDtypeStruct((16, 2, 80), F32),...]
    unnamed x1 -> x15, local copies, waits for them, and re-layouts: 1.32 us -> 1.33 us
where the time goes in v3:
time: 56.7 us; the launch traced here: 56.5 us
  Pallas kernels  55.1 us (97%)
  local copies, waits for them, and re-layouts  1.33 us (2%)
    pallas_call x1, Pallas kernels, body(): pl.pallas_call(kernel, out_shape=jax.ShapeDtypeStruct((16, 2, 80), F32),...  55.1 us
    unnamed x15, local copies, waits for them, and re-layouts  1.33 us

profile of v3, /device:TPU:1, one launch (start us, length us, event | category | flops | bytes accessed | tf_op | source)
XLA Modules:
  0.0 56.5 jit_solution(6465874828851276272)
XLA Ops:
  0.0 0.0 copy-start
  0.0 0.0 copy-start.6
  0.0 0.0 copy-start.2
  0.0 0.0 copy-start.4
  0.0 0.0 copy-start.5
  0.0 0.0 copy-start.1
  0.0 0.0 copy-start.3
  0.0 0.6 %copy-done = bf16[2,2,8,128]{3,2,1,0:T(8,128)(2,1)S(1)} copy-done((bf16[2,2,8,128]{3,2,1,0:T(8,128)(2,1)S(1)}, bf16[2,2,8,128]{3,2,1,0:T(8,128)(2,1)}, u32[]{:S(2)}) %copy-start) | copy-done | bytes 8216
  0.7 0.0 copy-done.6
  0.7 0.0 copy-done.2
  0.7 0.0 copy-done.4
  0.7 0.0 copy-done.5
  0.7 0.0 copy-done.1
  0.8 0.0 copy-done.3
  0.8 55.1 %shard_map.136 = f32[16,2,80]{2,1,0:T(2,128)S(1)} custom-call(bf16[32,128]{1,0:T(8,128)(2,1)S(1)} %bitcast.11, bf16[256,128]{1,0:T(8,128)(2,1)} %bitcast.20, bf16[256,128]{1,0:T(8,128)(2,1)} %bitcast.21, bf16[512,128]{1,0:T(8,128)(2,1)} %bitcast.16, bf16[512,128]{1,0:T(8,128)(2,1)} %bitcast.17, bf16[2,256,128]{2,1,0:T(8,128)(2,1)} %bitcast.18, ...), custom_call_target="tpu_custom_call" | custom-call | tf_op jit(solution)/shard_map/pallas_call | solution.py:404
  55.9 0.6 %copy.16 = f32[16,2,80]{2,1,0:T(2,128)} copy(f32[16,2,80]{2,1,0:T(2,128)S(1)} %shard_map.136) | data formatting | bytes 20480
Async XLA Ops:
  0.0 0.7 %copy-start = (bf16[2,2,8,128]{3,2,1,0:T(8,128)(2,1)S(1)}, bf16[2,2,8,128]{3,2,1,0:T(8,128)(2,1)}, u32[]{:S(2)}) copy-start(bf16[2,2,8,128]{3,2,1,0:T(8,128)(2,1)} %param.14) | copy-start | bytes 24580
  0.0 0.7 %copy-start.6 = (s32[2]{0:T(128)S(1)}, s32[2]{0:T(128)}, u32[]{:S(2)}) copy-start(s32[2]{0:T(128)} %cont_len_ref.1) | copy-start | bytes 28
  0.0 0.7 %copy-start.2 = (bf16[2,2,1,128]{3,1,2,0:T(2,128)(2,1)S(1)}, bf16[2,2,1,128]{3,1,2,0:T(2,128)(2,1)}, u32[]{:S(2)}) copy-start(bf16[2,2,1,128]{3,1,2,0:T(2,128)(2,1)} %param.16) | copy-start | bytes 3076
  0.0 0.7 %copy-start.4 = (s32[16]{0:T(128)S(1)}, s32[16]{0:T(128)}, u32[]{:S(2)}) copy-start(s32[16]{0:T(128)} %group_prompt_ref.1) | copy-start | bytes 196
  0.0 0.7 %copy-start.5 = (s32[16]{0:T(128)S(1)}, s32[16]{0:T(128)}, u32[]{:S(2)}) copy-start(s32[16]{0:T(128)} %prompt_len_ref.1) | copy-start | bytes 196
  0.0 0.7 %copy-start.1 = (bf16[2,2,1,128]{3,1,2,0:T(2,128)(2,1)S(1)}, bf16[2,2,1,128]{3,1,2,0:T(2,128)(2,1)}, u32[]{:S(2)}) copy-start(bf16[2,2,1,128]{3,1,2,0:T(2,128)(2,1)} %param.15) | copy-start | bytes 3076
  0.0 0.7 %copy-start.3 = (s32[128]{0:T(128)S(1)}, s32[128]{0:T(128)}, u32[]{:S(2)}) copy-start(s32[128]{0:T(128)} %param.25) | copy-start | bytes 1540

commit v4 on v3

v4 whole, which is shorter than its diff:
```python
import functools
import math

import jax
import jax.numpy as jnp
from jax import lax
from jax.experimental import pallas as pl
from jax.experimental.pallas import tpu as pltpu
from jax.sharding import PartitionSpec as P

NEG = -1e30
MESH = pl.DeviceIdType.MESH
F32, BF16 = jnp.float32, jnp.bfloat16
NX, NZ, NC, NY = 4, 8, 2, 8
CHIPS = NX * NZ
ROWS = 32
HD = 128
GROUP = 8
SCALING = 1.0 / math.sqrt(HD)


def dot(a, b):
    return jnp.dot(a, b, preferred_element_type=F32)


def dot_nt(a, b):
    return lax.dot_general(a, b, (((1,), (1,)), ((), ())), preferred_element_type=F32)


def iota(shape, axis):
    return lax.broadcasted_iota(jnp.int32, shape, axis)


def loop(low, high, step):
    def run(k, carry):
        step(k)
        return carry

    lax.fori_loop(low, high, run, 0)


def remote(src, dst, send_sem, recv_sem, chip, y, core):
    return pltpu.make_async_remote_copy(
        src_ref=src,
        dst_ref=dst,
        send_sem=send_sem,
        recv_sem=recv_sem,
        device_id={"seq": chip * 2 + core, "kvh": y},
        device_id_type=MESH,
    )


def with_ones(values):
    flipped = jnp.transpose(values.astype(F32))
    return jnp.concatenate([flipped, jnp.ones((16, values.shape[0]), F32)], axis=0).astype(BF16)


X_STEPS, Z_STEPS, Y_STEPS = (2, 1, 3, 0), (4, 3, 5, 2, 6, 1, 7, 0), (4, 3, 5, 2, 6, 1, 7, 0)
FAR_FIRST = [(dx, dz) for dx in X_STEPS for dz in Z_STEPS if dx or dz]


def join(peaks, parts):
    top = functools.reduce(jnp.maximum, peaks)
    total = None
    for peak, part in zip(peaks, parts):
        term = jnp.exp(peak - top) * part
        total = term if total is None else total + term
    stats = jnp.where(iota((8, 256), 0) == 1, top, total[128:136])
    return total[0:128], stats


def kernel(
    q_in,
    pk_in,
    pv_in,
    sk_in,
    sv_in,
    ck_in,
    cv_in,
    w_in,
    nk_ref,
    nv_ref,
    cont_prompt_ref,
    group_prompt_ref,
    prompt_len_ref,
    cont_len_ref,
    out_ref,
    q_line,
    keys,
    values,
    ck,
    cv,
    wt,
    parts,
    z_send,
    z_recv,
    att,
    att_f32,
    flat,
    y_send,
    y_recv,
    own_sem,
    w_ss,
    w_rs,
    kv_ss,
    kv_rs,
    fw_ss,
    fw_rs,
    col_sem,
    q_ss,
    q_rs,
    z_ss,
    z_rs,
    a_ss,
    a_rs,
    y_ss,
    y_rs,
):
    seq = lax.axis_index("seq")
    y = lax.axis_index("kvh")
    chip, c = seq // 2, seq % 2
    x, z = chip // NZ, chip % NZ
    other = 1 - c
    yc = y * 2 + c
    x_at = [lax.rem(x + d, NX) for d in range(NX)]
    x_to = [at * NZ for at in x_at]
    z_to = [lax.rem(z + d, NZ) for d in range(NZ)]
    y_to = [lax.rem(y + d, NY) for d in range(NY)]

    barrier = pltpu.get_barrier_semaphore()

    def greet(to_chip, to_y, to_c, sem=barrier):
        pl.semaphore_signal(
            sem, inc=1, device_id={"seq": to_chip * 2 + to_c, "kvh": to_y}, device_id_type=MESH
        )

    for dz in Z_STEPS[:-1]:
        greet(x_to[0] + z_to[dz], y, c)
    for dx in X_STEPS[:-1]:
        greet(x_to[dx] + z, y, c)
    for dy in (2, 6, 1, 7):
        greet(chip, y_to[dy], c)
        greet(chip, y_to[dy], other)
    greet(chip, y, other)

    local = [
        pltpu.make_async_copy(src, dst, own_sem.at[n])
        for n, (src, dst) in enumerate(
            [
                (q_in, q_line.at[z]),
                (pk_in, keys.at[x, c, pl.ds(0, 256)]),
                (sk_in, keys.at[x, c, pl.ds(256, 512)]),
                (pv_in, values.at[x, c, pl.ds(0, 256)]),
                (sv_in, values.at[x, c, pl.ds(256, 512)]),
                (ck_in, ck),
                (cv_in, cv),
                (w_in, wt.at[c, pl.ds(0, 80)]),
            ]
        )
    ]
    for copy in local:
        copy.start()
    for copy in local:
        copy.wait()
    pl.semaphore_wait(barrier, 19)

    def arrived(ref, sem):
        remote(ref, ref, q_ss, sem, chip, y, other).wait_recv()

    def left(ref, sem):
        remote(ref, ref, sem, q_rs, chip, y, other).wait_send()

    def kv_send(buffer, d, n, to):
        block = buffer.at[x_at[d], c]
        remote(block, block, kv_ss, kv_rs.at[n], x_to[to] + z, y, c).start()

    def to_core(buffer, d):
        block = buffer.at[x_at[d], c]
        remote(block, block, fw_ss, fw_rs.at[d], chip, y, other).start()

    kv_send(keys, 0, 0, 1)
    kv_send(values, 0, 1, 3)
    for dz in Z_STEPS[:-1]:
        block = q_line.at[z]
        remote(block, block, q_ss, q_rs, x_to[0] + z_to[dz], y, c).start()
    kv_send(values, 0, 2, 1)
    kv_send(keys, 0, 3, 3)
    to_core(keys, 0)
    to_core(values, 0)
    weights_swap = remote(
        wt.at[c, pl.ds(0, 80)], wt.at[c, pl.ds(0, 80)], w_ss, w_rs, chip, y, other
    )
    weights_swap.start()
    for dy in (2, 6):
        greet(chip, y_to[dy], c, col_sem)

    wt[:, 80:, :] = jnp.zeros((2, 48, wt.shape[2]), BF16)
    lane = iota((128, 256), 1)
    cont = (x * NZ + lane // ROWS) * 4 + c * 2 + (lane % ROWS) // 16
    widen = jnp.where(iota((128, 256), 0) == cont, 1.0, 0.0).astype(BF16)
    prompts = jnp.broadcast_to(cont_prompt_ref[...].astype(F32), (8, 128)).astype(BF16)
    prompt_of = dot(prompts, widen)[0:1]

    q_own = q_line[z]
    first = iota((ROWS, 1), 0) < 16
    past0 = dot_nt(q_own, ck[0]) * SCALING
    past1 = dot_nt(q_own, ck[1]) * SCALING
    lengths = jnp.where(first, cont_len_ref[0], cont_len_ref[1])
    past = jnp.where(iota(past0.shape, 1) < lengths, jnp.where(first, past0, past1), NEG)
    fresh_pad = jnp.zeros((12, HD), F32)
    nk = jnp.concatenate([nk_ref[0].astype(F32), nk_ref[1].astype(F32), fresh_pad], axis=0).astype(BF16)
    nv = jnp.concatenate([nv_ref[0].astype(F32), nv_ref[1].astype(F32), fresh_pad], axis=0).astype(BF16)
    fresh = dot_nt(q_own, nk) * SCALING
    row, col = iota(fresh.shape, 0), iota(fresh.shape, 1)
    seen = (col // 2 == row // 16) & (col % 2 <= (row // 8) % 2)
    fresh = jnp.where(seen, fresh, NEG)
    own_peak = jnp.maximum(jnp.max(past, axis=1, keepdims=True), jnp.max(fresh, axis=1, keepdims=True))
    past_w = jnp.exp(past - own_peak).astype(BF16)
    fresh_w = jnp.exp(fresh - own_peak).astype(BF16)
    own_total = jnp.sum(past_w.astype(F32), axis=1, keepdims=True) + jnp.sum(
        fresh_w.astype(F32), axis=1, keepdims=True
    )
    own_part = jnp.where(first, dot(past_w, cv[0]), dot(past_w, cv[1])) + dot(fresh_w, nv)
    def unit(n, at, core):
        prompt = group_prompt_ref[(at * NZ + z) // 2]
        length = prompt_len_ref[prompt]
        rows = q_line[...].reshape(NZ * ROWS, HD)
        scores = dot_nt(keys[at, core], rows) * SCALING
        flipped = with_ones(values[at, core])
        place = ((z % 2) * 2 + core) * 512 + iota((512, 1), 0)
        store = jnp.where(place < length, scores[256:], NEG)
        prefix_peak = jnp.max(scores[:256], axis=0, keepdims=True)
        store_peak = jnp.max(store, axis=0, keepdims=True)
        prefix = dot(flipped[:, :256], jnp.exp(scores[:256] - prefix_peak).astype(BF16))
        store = dot(flipped[:, 256:], jnp.exp(store - store_peak).astype(BF16))
        mine = prompt_of == jnp.full((1, 256), prompt, jnp.int32).astype(F32)
        part, stats = join([prefix_peak, jnp.where(mine, store_peak, NEG)], [prefix[0:136], store[0:136]])
        parts[n, 0:128] = part
        parts[n, 128:136] = stats

    def from_core(d):
        arrived(keys.at[0], fw_rs.at[d])

    arrived(keys.at[0, 0], kv_rs.at[0])
    kv_send(keys, 3, 4, 1)
    to_core(keys, 3)
    arrived(keys.at[0, 0], kv_rs.at[1])
    kv_send(values, 1, 5, 3)
    to_core(values, 1)
    arrived(q_line.at[pl.ds(0, NZ - 1)], q_rs)
    unit(0, x, c)
    from_core(0)
    unit(1, x, other)
    arrived(keys.at[0, 0], kv_rs.at[2])
    to_core(values, 3)
    arrived(keys.at[0, 0], kv_rs.at[3])
    to_core(keys, 1)
    loop(0, 2, lambda i: unit(2 + i, lax.rem(x + 3 - 2 * i, NX), c))
    from_core(3)
    from_core(1)
    loop(0, 2, lambda i: unit(4 + i, lax.rem(x + 3 - 2 * i, NX), other))
    arrived(keys.at[0, 0], kv_rs.at[4])
    to_core(keys, 2)
    arrived(keys.at[0, 0], kv_rs.at[5])
    to_core(values, 2)
    unit(6, x_at[2], c)
    from_core(2)
    unit(7, x_at[2], other)
    part, stats = join([parts[n, 129:130] for n in range(8)], [parts[n] for n in range(8)])

    by_row = jnp.transpose(part)
    for t in range(NZ):
        half = stats[:, (t // 4) * 128 : (t // 4 + 1) * 128]
        turned = half if t % 4 == 0 else pltpu.roll(half, 128 - (t % 4) * ROWS, 1)
        z_send[t, 0:ROWS] = by_row[t * ROWS : (t + 1) * ROWS]
        z_send[t, ROWS : ROWS + 8] = turned

    for dz in Z_STEPS[:-1]:
        to = z_to[dz]
        remote(z_send.at[to], z_recv.at[z], z_ss, z_rs, x_to[0] + to, y, c).start()
    z_recv[z] = z_send[z]
    left(q_line.at[pl.ds(0, NZ - 1)], q_ss)
    left(keys.at[pl.ds(0, 3)], kv_ss)
    left(keys, fw_ss)
    weights_swap.wait()
    pl.semaphore_wait(col_sem, 2)
    arrived(z_recv.at[pl.ds(0, NZ - 1)], z_rs)

    side = jnp.concatenate(
        [z_recv[s, ROWS + 1 : ROWS + 2] for s in range(NZ)]
        + [z_recv[s, ROWS : ROWS + 1] for s in range(NZ)]
        + [jnp.zeros((112, 128), F32)],
        axis=0,
    )
    side = jnp.transpose(side)[0:ROWS]
    top = jnp.maximum(jnp.max(side[:, 0:NZ], axis=1, keepdims=True), own_peak)
    own_factor = jnp.exp(own_peak - top)
    total, weighted = own_factor * own_total, own_factor * own_part
    for s in range(NZ):
        factor = jnp.exp(side[:, s : s + 1] - top)
        total = total + factor * side[:, NZ + s : NZ + s + 1]
        weighted = weighted + factor * z_recv[s, 0:ROWS]
    att[chip] = (weighted / total).astype(BF16)

    for dx, dz in FAR_FIRST:
        block = att.at[chip]
        remote(block, block, a_ss, a_rs, x_to[dx] + z_to[dz], y, c).start()
    left(z_send.at[pl.ds(0, NZ - 1)], z_ss)
    arrived(att.at[pl.ds(0, CHIPS - 1)], a_rs)

    att_f32[...] = att[...].reshape(CHIPS * ROWS, HD).astype(F32)
    for h in range(GROUP):
        flat[:, h * HD : (h + 1) * HD] = att_f32[pl.ds(h, 128, stride=GROUP), :].astype(BF16)
    for b in range(2):
        y_send[b] = dot_nt(flat[...], wt[b]).reshape(NY, 16, 128)
    for dy in Y_STEPS:
        for dc in (1, 0):
            if dy or dc:
                to_y, to_c = y_to[dy], other if dc else c
                remote(y_send.at[to_c, to_y], y_recv.at[yc], y_ss, y_rs, chip, to_y, to_c).start()
    y_recv[yc] = y_send[c, y]
    left(att.at[pl.ds(0, CHIPS - 1)], a_ss)
    arrived(y_recv.at[pl.ds(0, 15)], y_rs)
    for b in range(2):
        summed = functools.reduce(jnp.add, [y_recv[n * 2 + b] for n in range(NY)])
        for n in range(4):
            for i in range(2):
                out_ref[n * 4 + b * 2 + i] = summed[n * 4 + i * 2 : n * 4 + i * 2 + 2, 0:80]

    left(y_recv.at[pl.ds(0, 15)], y_ss)


def body(
    queries,
    new_keys,
    new_values,
    prefix_keys,
    prefix_values,
    prompt_keys,
    prompt_values,
    cache_keys,
    cache_values,
    group_prompt,
    prompt_len,
    cont_prompt,
    cont_len,
    out_weight,
):
    anywhere = pl.BlockSpec(memory_space=pl.ANY)
    vmem = pl.BlockSpec(memory_space=pltpu.VMEM)
    smem = pl.BlockSpec(memory_space=pltpu.SMEM)
    dma = pltpu.SemaphoreType.DMA
    return pl.pallas_call(
        kernel,
        out_shape=jax.ShapeDtypeStruct((16, 2, 80), F32),
        in_specs=[anywhere] * 8 + [vmem] * 3 + [smem] * 3,
        out_specs=vmem,
        scratch_shapes=[
            pltpu.VMEM((NZ, ROWS, HD), BF16),
            pltpu.VMEM((NX, 2, 768, HD), BF16),
            pltpu.VMEM((NX, 2, 768, HD), BF16),
            pltpu.VMEM((2, 256, HD), BF16),
            pltpu.VMEM((2, 256, HD), BF16),
            pltpu.VMEM((2, 128, 1024), BF16),
            pltpu.VMEM((8, 136, 256), F32),
            pltpu.VMEM((NZ, 40, 128), F32),
            pltpu.VMEM((NZ, 40, 128), F32),
            pltpu.VMEM((CHIPS, ROWS, HD), BF16),
            pltpu.VMEM((CHIPS * ROWS, HD), F32),
            pltpu.VMEM((128, 1024), BF16),
            pltpu.VMEM((2, NY, 16, 128), F32),
            pltpu.VMEM((16, 16, 128), F32),
            dma((8,)),
            dma,
            dma,
            dma,
            dma((6,)),
            dma,
            dma((NX,)),
            pltpu.SemaphoreType.REGULAR,
            dma,
            dma,
            dma,
            dma,
            dma,
            dma,
            dma,
            dma,
        ],
        compiler_params=pltpu.CompilerParams(
            collective_id=0, has_side_effects=True, vmem_limit_bytes=55168 << 10
        ),
    )(
        queries.reshape(ROWS, HD),
        prefix_keys[:, 0, :],
        prefix_values[:, 0, :],
        prompt_keys[:, 0, :],
        prompt_values[:, 0, :],
        cache_keys[:, :, 0, :],
        cache_values[:, :, 0, :],
        out_weight.T,
        new_keys[:, :, 0, :],
        new_values[:, :, 0, :],
        cont_prompt.reshape(1, 128),
        group_prompt,
        prompt_len,
        cont_len,
    )


def solution(mesh):
    in_specs = (
        P("seq", None, "kvh", None),
        P("seq", None, "kvh", None),
        P("seq", None, "kvh", None),
        P("seq", "kvh", None),
        P("seq", "kvh", None),
        P("seq", "kvh", None),
        P("seq", "kvh", None),
        P("seq", None, "kvh", None),
        P("seq", None, "kvh", None),
        P(),
        P(),
        P(),
        P("seq"),
        P("kvh", "seq"),
    )
    out_specs = P("kvh", None, "seq")
    return jax.shard_map(body, mesh=mesh, in_specs=in_specs, out_specs=out_specs, check_vma=False)
```

time: 56.7 us -> 55.8 us (0.984)
  Pallas kernels: 55.1 us -> 54.2 us
    pallas_call x1, Pallas kernels: 55.1 us -> 54.2 us  [body(): pl.pallas_call(kernel, out_shape=jax.ShapeDtypeStruct((16, 2, 80), F32),...]
where the time goes in v4:
time: 55.8 us; the launch traced here: 55.6 us
  Pallas kernels  54.2 us (97%)
  local copies, waits for them, and re-layouts  1.33 us (2%)
    pallas_call x1, Pallas kernels, body(): pl.pallas_call(kernel, out_shape=jax.ShapeDtypeStruct((16, 2, 80), F32),...  54.2 us
    unnamed x15, local copies, waits for them, and re-layouts  1.33 us

profile of v4, /device:TPU:1, one launch (start us, length us, event | category | flops | bytes accessed | tf_op | source)
XLA Modules:
  0.0 55.6 jit_solution(11951190034612271959)
XLA Ops:
  0.0 0.0 copy-start
  0.0 0.0 copy-start.6
  0.0 0.0 copy-start.2
  0.0 0.0 copy-start.4
  0.0 0.0 copy-start.5
  0.0 0.0 copy-start.1
  0.0 0.0 copy-start.3
  0.0 0.6 %copy-done = bf16[2,2,8,128]{3,2,1,0:T(8,128)(2,1)S(1)} copy-done((bf16[2,2,8,128]{3,2,1,0:T(8,128)(2,1)S(1)}, bf16[2,2,8,128]{3,2,1,0:T(8,128)(2,1)}, u32[]{:S(2)}) %copy-start) | copy-done | bytes 8216
  0.7 0.0 copy-done.6
  0.7 0.0 copy-done.2
  0.7 0.0 copy-done.4
  0.7 0.0 copy-done.5
  0.7 0.0 copy-done.1
  0.8 0.0 copy-done.3
  0.8 54.2 %shard_map.136 = f32[16,2,80]{2,1,0:T(2,128)S(1)} custom-call(bf16[32,128]{1,0:T(8,128)(2,1)S(1)} %bitcast.11, bf16[256,128]{1,0:T(8,128)(2,1)} %bitcast.20, bf16[256,128]{1,0:T(8,128)(2,1)} %bitcast.21, bf16[512,128]{1,0:T(8,128)(2,1)} %bitcast.16, bf16[512,128]{1,0:T(8,128)(2,1)} %bitcast.17, bf16[2,256,128]{2,1,0:T(8,128)(2,1)} %bitcast.18, ...), custom_call_target="tpu_custom_call" | custom-call | tf_op jit(solution)/shard_map/pallas_call | solution.py:353
  55.0 0.6 %copy.16 = f32[16,2,80]{2,1,0:T(2,128)} copy(f32[16,2,80]{2,1,0:T(2,128)S(1)} %shard_map.136) | data formatting | bytes 20480
Async XLA Ops:
  0.0 0.7 %copy-start = (bf16[2,2,8,128]{3,2,1,0:T(8,128)(2,1)S(1)}, bf16[2,2,8,128]{3,2,1,0:T(8,128)(2,1)}, u32[]{:S(2)}) copy-start(bf16[2,2,8,128]{3,2,1,0:T(8,128)(2,1)} %param.14) | copy-start | bytes 24580
  0.0 0.7 %copy-start.6 = (s32[2]{0:T(128)S(1)}, s32[2]{0:T(128)}, u32[]{:S(2)}) copy-start(s32[2]{0:T(128)} %cont_len_ref.1) | copy-start | bytes 28
  0.0 0.7 %copy-start.2 = (bf16[2,2,1,128]{3,1,2,0:T(2,128)(2,1)S(1)}, bf16[2,2,1,128]{3,1,2,0:T(2,128)(2,1)}, u32[]{:S(2)}) copy-start(bf16[2,2,1,128]{3,1,2,0:T(2,128)(2,1)} %param.16) | copy-start | bytes 3076
  0.0 0.7 %copy-start.4 = (s32[16]{0:T(128)S(1)}, s32[16]{0:T(128)}, u32[]{:S(2)}) copy-start(s32[16]{0:T(128)} %group_prompt_ref.1) | copy-start | bytes 196
  0.0 0.7 %copy-start.5 = (s32[16]{0:T(128)S(1)}, s32[16]{0:T(128)}, u32[]{:S(2)}) copy-start(s32[16]{0:T(128)} %prompt_len_ref.1) | copy-start | bytes 196
  0.0 0.7 %copy-start.1 = (bf16[2,2,1,128]{3,1,2,0:T(2,128)(2,1)S(1)}, bf16[2,2,1,128]{3,1,2,0:T(2,128)(2,1)}, u32[]{:S(2)}) copy-start(bf16[2,2,1,128]{3,1,2,0:T(2,128)(2,1)} %param.15) | copy-start | bytes 3076
  0.0 0.7 %copy-start.3 = (s32[128]{0:T(128)S(1)}, s32[128]{0:T(128)}, u32[]{:S(2)}) copy-start(s32[128]{0:T(128)} %param.25) | copy-start | bytes 1540

commit v5 on v4

--- a/solution.py
+++ b/solution.py
@@ -134,10 +134,10 @@
             sem, inc=1, device_id={"seq": to_chip * 2 + to_c, "kvh": to_y}, device_id_type=MESH
         )
 
-    for dz in Z_STEPS[:-1]:
+    for dx in (1, 3):
+        greet(x_to[dx] + z, y, c)
+    for dz in (2, 6, 1, 7):
         greet(x_to[0] + z_to[dz], y, c)
-    for dx in X_STEPS[:-1]:
-        greet(x_to[dx] + z, y, c)
     for dy in (2, 6, 1, 7):
         greet(chip, y_to[dy], c)
         greet(chip, y_to[dy], other)
@@ -160,17 +160,20 @@
     ]
     for copy in local:
         copy.start()
-    for copy in local:
-        copy.wait()
-    pl.semaphore_wait(barrier, 19)
+    pl.semaphore_wait(barrier, 15)
 
     def arrived(ref, sem):
         remote(ref, ref, q_ss, sem, chip, y, other).wait_recv()
 
     def left(ref, sem):
-        remote(ref, ref, sem, q_rs, chip, y, other).wait_send()
-
-    def kv_send(buffer, d, n, to):
+        remote(ref, ref, sem, q_rs.at[0], chip, y, other).wait_send()
+
+    def own_to_x(prefix, store, buffer, n, to):
+        for src, first, count in ((store, 256, 512), (prefix, 0, 256)):
+            dst = buffer.at[x, c, pl.ds(first, count)]
+            remote(src, dst, kv_ss, kv_rs.at[n], x_to[to] + z, y, c).start()
+
+    def relay(buffer, d, n, to):
         block = buffer.at[x_at[d], c]
         remote(block, block, kv_ss, kv_rs.at[n], x_to[to] + z, y, c).start()
 
@@ -178,13 +181,19 @@
         block = buffer.at[x_at[d], c]
         remote(block, block, fw_ss, fw_rs.at[d], chip, y, other).start()
 
-    kv_send(keys, 0, 0, 1)
-    kv_send(values, 0, 1, 3)
-    for dz in Z_STEPS[:-1]:
-        block = q_line.at[z]
-        remote(block, block, q_ss, q_rs, x_to[0] + z_to[dz], y, c).start()
-    kv_send(values, 0, 2, 1)
-    kv_send(keys, 0, 3, 3)
+    def q_send(dz, n, to):
+        block = q_line.at[z_to[dz]]
+        src = block if dz else q_in
+        remote(src, block, q_ss, q_rs.at[n], x_to[0] + z_to[to], y, c).start()
+
+    own_to_x(pk_in, sk_in, keys, 0, 1)
+    own_to_x(pv_in, sv_in, values, 1, 3)
+    for dz in (2, 6, 1, 7):
+        q_send(0, 0, dz)
+    own_to_x(pv_in, sv_in, values, 2, 1)
+    own_to_x(pk_in, sk_in, keys, 3, 3)
+    for copy in local:
+        copy.wait()
     to_core(keys, 0)
     to_core(values, 0)
     weights_swap = remote(
@@ -241,13 +250,17 @@
     def from_core(d):
         arrived(keys.at[0], fw_rs.at[d])
 
+    arrived(q_line.at[pl.ds(0, 4)], q_rs.at[0])
+    q_send(1, 1, 6)
+    q_send(2, 1, 6)
+    q_send(7, 1, 2)
     arrived(keys.at[0, 0], kv_rs.at[0])
-    kv_send(keys, 3, 4, 1)
+    relay(keys, 3, 4, 1)
     to_core(keys, 3)
     arrived(keys.at[0, 0], kv_rs.at[1])
-    kv_send(values, 1, 5, 3)
+    relay(values, 1, 5, 3)
     to_core(values, 1)
-    arrived(q_line.at[pl.ds(0, NZ - 1)], q_rs)
+    arrived(q_line.at[pl.ds(0, 3)], q_rs.at[1])
     unit(0, x, c)
     from_core(0)
     unit(1, x, other)
@@ -273,7 +286,7 @@
         half = stats[:, (t // 4) * 128 : (t // 4 + 1) * 128]
         turned = half if t % 4 == 0 else pltpu.roll(half, 128 - (t % 4) * ROWS, 1)
         z_send[t, 0:ROWS] = by_row[t * ROWS : (t + 1) * ROWS]
-        z_send[t, ROWS : ROWS + 8] = turned
+        z_send[t, ROWS : ROWS + 2] = turned[0:2]
 
     for dz in Z_STEPS[:-1]:
         to = z_to[dz]
@@ -311,13 +324,11 @@
     att_f32[...] = att[...].reshape(CHIPS * ROWS, HD).astype(F32)
     for h in range(GROUP):
         flat[:, h * HD : (h + 1) * HD] = att_f32[pl.ds(h, 128, stride=GROUP), :].astype(BF16)
-    for b in range(2):
-        y_send[b] = dot_nt(flat[...], wt[b]).reshape(NY, 16, 128)
-    for dy in Y_STEPS:
-        for dc in (1, 0):
-            if dy or dc:
-                to_y, to_c = y_to[dy], other if dc else c
-                remote(y_send.at[to_c, to_y], y_recv.at[yc], y_ss, y_rs, chip, to_y, to_c).start()
+    for to_c in (other, c):
+        y_send[to_c] = dot_nt(flat[...], wt[to_c]).reshape(NY, 16, 128)
+        for dy in Y_STEPS if to_c is other else Y_STEPS[:-1]:
+            to_y = y_to[dy]
+            remote(y_send.at[to_c, to_y], y_recv.at[yc], y_ss, y_rs, chip, to_y, to_c).start()
     y_recv[yc] = y_send[c, y]
     left(att.at[pl.ds(0, CHIPS - 1)], a_ss)
     arrived(y_recv.at[pl.ds(0, 15)], y_rs)
@@ -363,8 +374,8 @@
             pltpu.VMEM((2, 256, HD), BF16),
             pltpu.VMEM((2, 128, 1024), BF16),
             pltpu.VMEM((8, 136, 256), F32),
-            pltpu.VMEM((NZ, 40, 128), F32),
-            pltpu.VMEM((NZ, 40, 128), F32),
+            pltpu.VMEM((NZ, 34, 128), F32),
+            pltpu.VMEM((NZ, 34, 128), F32),
             pltpu.VMEM((CHIPS, ROWS, HD), BF16),
             pltpu.VMEM((CHIPS * ROWS, HD), F32),
             pltpu.VMEM((128, 1024), BF16),
@@ -379,7 +390,7 @@
             dma((NX,)),
             pltpu.SemaphoreType.REGULAR,
             dma,
-            dma,
+            dma((2,)),
             dma,
             dma,
             dma,

time: 55.8 us -> 53.5 us (0.959)
  Pallas kernels: 54.2 us -> 52 us
    pallas_call x1, Pallas kernels: 54.2 us -> 52 us  [body(): pl.pallas_call(kernel, out_shape=jax.ShapeDtypeStruct((16, 2, 80), F32),...]
where the time goes in v5:
time: 53.5 us; the launch traced here: 53.4 us
  Pallas kernels  52 us (97%)
  local copies, waits for them, and re-layouts  1.33 us (2%)
    pallas_call x1, Pallas kernels, body(): pl.pallas_call(kernel, out_shape=jax.ShapeDtypeStruct((16, 2, 80), F32),...  52 us
    unnamed x15, local copies, waits for them, and re-layouts  1.33 us

profile of v5, /device:TPU:1, one launch (start us, length us, event | category | flops | bytes accessed | tf_op | source)
XLA Modules:
  0.0 53.4 jit_solution(309689003579087094)
XLA Ops:
  0.0 0.0 copy-start
  0.0 0.0 copy-start.6
  0.0 0.0 copy-start.2
  0.0 0.0 copy-start.4
  0.0 0.0 copy-start.5
  0.0 0.0 copy-start.1
  0.0 0.0 copy-start.3
  0.0 0.6 %copy-done = bf16[2,2,8,128]{3,2,1,0:T(8,128)(2,1)S(1)} copy-done((bf16[2,2,8,128]{3,2,1,0:T(8,128)(2,1)S(1)}, bf16[2,2,8,128]{3,2,1,0:T(8,128)(2,1)}, u32[]{:S(2)}) %copy-start) | copy-done | bytes 8216
  0.7 0.0 copy-done.6
  0.7 0.0 copy-done.2
  0.7 0.0 copy-done.4
  0.7 0.0 copy-done.5
  0.7 0.0 copy-done.1
  0.8 0.0 copy-done.3
  0.8 52.0 %shard_map.136 = f32[16,2,80]{2,1,0:T(2,128)S(1)} custom-call(bf16[32,128]{1,0:T(8,128)(2,1)S(1)} %bitcast.11, bf16[256,128]{1,0:T(8,128)(2,1)} %bitcast.20, bf16[256,128]{1,0:T(8,128)(2,1)} %bitcast.21, bf16[512,128]{1,0:T(8,128)(2,1)} %bitcast.16, bf16[512,128]{1,0:T(8,128)(2,1)} %bitcast.17, bf16[2,256,128]{2,1,0:T(8,128)(2,1)} %bitcast.18, ...), custom_call_target="tpu_custom_call" | custom-call | tf_op jit(solution)/shard_map/pallas_call | solution.py:364
  52.8 0.6 %copy.16 = f32[16,2,80]{2,1,0:T(2,128)} copy(f32[16,2,80]{2,1,0:T(2,128)S(1)} %shard_map.136) | data formatting | bytes 20480
Async XLA Ops:
  0.0 0.7 %copy-start = (bf16[2,2,8,128]{3,2,1,0:T(8,128)(2,1)S(1)}, bf16[2,2,8,128]{3,2,1,0:T(8,128)(2,1)}, u32[]{:S(2)}) copy-start(bf16[2,2,8,128]{3,2,1,0:T(8,128)(2,1)} %param.14) | copy-start | bytes 24580
  0.0 0.7 %copy-start.6 = (s32[2]{0:T(128)S(1)}, s32[2]{0:T(128)}, u32[]{:S(2)}) copy-start(s32[2]{0:T(128)} %cont_len_ref.1) | copy-start | bytes 28
  0.0 0.7 %copy-start.2 = (bf16[2,2,1,128]{3,1,2,0:T(2,128)(2,1)S(1)}, bf16[2,2,1,128]{3,1,2,0:T(2,128)(2,1)}, u32[]{:S(2)}) copy-start(bf16[2,2,1,128]{3,1,2,0:T(2,128)(2,1)} %param.16) | copy-start | bytes 3076
  0.0 0.7 %copy-start.4 = (s32[16]{0:T(128)S(1)}, s32[16]{0:T(128)}, u32[]{:S(2)}) copy-start(s32[16]{0:T(128)} %group_prompt_ref.1) | copy-start | bytes 196
  0.0 0.7 %copy-start.5 = (s32[16]{0:T(128)S(1)}, s32[16]{0:T(128)}, u32[]{:S(2)}) copy-start(s32[16]{0:T(128)} %prompt_len_ref.1) | copy-start | bytes 196
  0.0 0.7 %copy-start.1 = (bf16[2,2,1,128]{3,1,2,0:T(2,128)(2,1)S(1)}, bf16[2,2,1,128]{3,1,2,0:T(2,128)(2,1)}, u32[]{:S(2)}) copy-start(bf16[2,2,1,128]{3,1,2,0:T(2,128)(2,1)} %param.15) | copy-start | bytes 3076
  0.0 0.7 %copy-start.3 = (s32[128]{0:T(128)S(1)}, s32[128]{0:T(128)}, u32[]{:S(2)}) copy-start(s32[128]{0:T(128)} %param.25) | copy-start | bytes 1540

commit v6 on v5

--- a/solution.py
+++ b/solution.py
@@ -81,17 +81,23 @@
     nk_ref,
     nv_ref,
     cont_prompt_ref,
+    group_prompt_in,
+    prompt_len_in,
+    cont_len_in,
+    out_ref,
     group_prompt_ref,
     prompt_len_ref,
     cont_len_ref,
-    out_ref,
     q_line,
+    q_other,
     keys,
     values,
     ck,
     cv,
     wt,
     parts,
+    p_send,
+    p_recv,
     z_send,
     z_recv,
     att,
@@ -104,8 +110,8 @@
     w_rs,
     kv_ss,
     kv_rs,
-    fw_ss,
-    fw_rs,
+    swap_ss,
+    swap_rs,
     col_sem,
     q_ss,
     q_rs,
@@ -148,13 +154,16 @@
         for n, (src, dst) in enumerate(
             [
                 (q_in, q_line.at[z]),
-                (pk_in, keys.at[x, c, pl.ds(0, 256)]),
-                (sk_in, keys.at[x, c, pl.ds(256, 512)]),
-                (pv_in, values.at[x, c, pl.ds(0, 256)]),
-                (sv_in, values.at[x, c, pl.ds(256, 512)]),
+                (pk_in, keys.at[x, pl.ds(0, 256)]),
+                (sk_in, keys.at[x, pl.ds(256, 512)]),
+                (pv_in, values.at[x, pl.ds(0, 256)]),
+                (sv_in, values.at[x, pl.ds(256, 512)]),
                 (ck_in, ck),
                 (cv_in, cv),
                 (w_in, wt.at[c, pl.ds(0, 80)]),
+                (group_prompt_in, group_prompt_ref),
+                (prompt_len_in, prompt_len_ref),
+                (cont_len_in, cont_len_ref),
             ]
         )
     ]
@@ -169,17 +178,17 @@
         remote(ref, ref, sem, q_rs.at[0], chip, y, other).wait_send()
 
     def own_to_x(prefix, store, buffer, n, to):
-        for src, first, count in ((store, 256, 512), (prefix, 0, 256)):
-            dst = buffer.at[x, c, pl.ds(first, count)]
-            remote(src, dst, kv_ss, kv_rs.at[n], x_to[to] + z, y, c).start()
+        for src, start, count in ((store, 256, 512), (prefix, 0, 256)):
+            dst = buffer.at[x, pl.ds(start, count)]
+            remote(src, dst, kv_ss.at[n % 2], kv_rs.at[n], x_to[to] + z, y, c).start()
 
     def relay(buffer, d, n, to):
-        block = buffer.at[x_at[d], c]
-        remote(block, block, kv_ss, kv_rs.at[n], x_to[to] + z, y, c).start()
-
-    def to_core(buffer, d):
-        block = buffer.at[x_at[d], c]
-        remote(block, block, fw_ss, fw_rs.at[d], chip, y, other).start()
+        for m, start, count in ((n, 256, 512), (n + 2, 0, 256)):
+            block = buffer.at[x_at[d], pl.ds(start, count)]
+            remote(block, block, kv_ss.at[n % 2], kv_rs.at[m], x_to[to] + z, y, c).start()
+
+    def swap(src, dst, n):
+        return remote(src, dst, swap_ss.at[n], swap_rs.at[n], chip, y, other)
 
     def q_send(dz, n, to):
         block = q_line.at[z_to[dz]]
@@ -190,12 +199,10 @@
     own_to_x(pv_in, sv_in, values, 1, 3)
     for dz in (2, 6, 1, 7):
         q_send(0, 0, dz)
-    own_to_x(pv_in, sv_in, values, 2, 1)
-    own_to_x(pk_in, sk_in, keys, 3, 3)
+    own_to_x(pv_in, sv_in, values, 3, 1)
+    own_to_x(pk_in, sk_in, keys, 2, 3)
     for copy in local:
         copy.wait()
-    to_core(keys, 0)
-    to_core(values, 0)
     weights_swap = remote(
         wt.at[c, pl.ds(0, 80)], wt.at[c, pl.ds(0, 80)], w_ss, w_rs, chip, y, other
     )
@@ -205,10 +212,12 @@
 
     wt[:, 80:, :] = jnp.zeros((2, 48, wt.shape[2]), BF16)
     lane = iota((128, 256), 1)
-    cont = (x * NZ + lane // ROWS) * 4 + c * 2 + (lane % ROWS) // 16
-    widen = jnp.where(iota((128, 256), 0) == cont, 1.0, 0.0).astype(BF16)
     prompts = jnp.broadcast_to(cont_prompt_ref[...].astype(F32), (8, 128)).astype(BF16)
-    prompt_of = dot(prompts, widen)[0:1]
+    prompt_of = []
+    for core in (c, other):
+        cont = (x * NZ + lane // ROWS) * 4 + core * 2 + (lane % ROWS) // 16
+        widen = jnp.where(iota((128, 256), 0) == cont, 1.0, 0.0).astype(BF16)
+        prompt_of.append(dot(prompts, widen)[0:1])
 
     q_own = q_line[z]
     first = iota((ROWS, 1), 0) < 16
@@ -230,56 +239,70 @@
         fresh_w.astype(F32), axis=1, keepdims=True
     )
     own_part = jnp.where(first, dot(past_w, cv[0]), dot(past_w, cv[1])) + dot(fresh_w, nv)
-    def unit(n, at, core):
+    def rows_of(r):
+        return (q_other if r else q_line)[...].reshape(NZ * ROWS, HD)
+
+    def prefix_block(at, flipped, r):
+        scores = dot_nt(keys[at, 0:256], rows_of(r)) * SCALING
+        peak = jnp.max(scores, axis=0, keepdims=True)
+        return peak, dot(flipped, jnp.exp(scores - peak).astype(BF16))[0:136]
+
+    def store_block(at, flipped, r):
         prompt = group_prompt_ref[(at * NZ + z) // 2]
-        length = prompt_len_ref[prompt]
-        rows = q_line[...].reshape(NZ * ROWS, HD)
-        scores = dot_nt(keys[at, core], rows) * SCALING
-        flipped = with_ones(values[at, core])
-        place = ((z % 2) * 2 + core) * 512 + iota((512, 1), 0)
-        store = jnp.where(place < length, scores[256:], NEG)
-        prefix_peak = jnp.max(scores[:256], axis=0, keepdims=True)
-        store_peak = jnp.max(store, axis=0, keepdims=True)
-        prefix = dot(flipped[:, :256], jnp.exp(scores[:256] - prefix_peak).astype(BF16))
-        store = dot(flipped[:, 256:], jnp.exp(store - store_peak).astype(BF16))
-        mine = prompt_of == jnp.full((1, 256), prompt, jnp.int32).astype(F32)
-        part, stats = join([prefix_peak, jnp.where(mine, store_peak, NEG)], [prefix[0:136], store[0:136]])
-        parts[n, 0:128] = part
-        parts[n, 128:136] = stats
-
-    def from_core(d):
-        arrived(keys.at[0], fw_rs.at[d])
+        place = ((z % 2) * 2 + c) * 512 + iota((512, 1), 0)
+        scores = dot_nt(keys[at, 256:768], rows_of(r)) * SCALING
+        scores = jnp.where(place < prompt_len_ref[prompt], scores, NEG)
+        peak = jnp.max(scores, axis=0, keepdims=True)
+        part = dot(flipped, jnp.exp(scores - peak).astype(BF16))[0:136]
+        mine = prompt_of[r] == jnp.full((1, 256), prompt, jnp.int32).astype(F32)
+        return jnp.where(mine, peak, NEG), part
+
+    def keep(ref, part, stats):
+        ref[0:128] = part
+        ref[128:136] = stats
+
+    def unit(n, at, row_sets):
+        flipped = with_ones(values[at])
+        for r in row_sets:
+            blocks = [prefix_block(at, flipped[:, :256], r), store_block(at, flipped[:, 256:], r)]
+            keep(parts.at[r, n], *join(*zip(*blocks)))
+
+    def joined(r, more):
+        kept = [(parts[r, n, 129:130], parts[r, n]) for n in range(4)]
+        return join(*zip(*(kept + more)))
 
     arrived(q_line.at[pl.ds(0, 4)], q_rs.at[0])
     q_send(1, 1, 6)
     q_send(2, 1, 6)
     q_send(7, 1, 2)
-    arrived(keys.at[0, 0], kv_rs.at[0])
+    arrived(keys.at[0], kv_rs.at[0])
     relay(keys, 3, 4, 1)
-    to_core(keys, 3)
-    arrived(keys.at[0, 0], kv_rs.at[1])
+    arrived(keys.at[0], kv_rs.at[1])
     relay(values, 1, 5, 3)
-    to_core(values, 1)
     arrived(q_line.at[pl.ds(0, 3)], q_rs.at[1])
-    unit(0, x, c)
-    from_core(0)
-    unit(1, x, other)
-    arrived(keys.at[0, 0], kv_rs.at[2])
-    to_core(values, 3)
-    arrived(keys.at[0, 0], kv_rs.at[3])
-    to_core(keys, 1)
-    loop(0, 2, lambda i: unit(2 + i, lax.rem(x + 3 - 2 * i, NX), c))
-    from_core(3)
-    from_core(1)
-    loop(0, 2, lambda i: unit(4 + i, lax.rem(x + 3 - 2 * i, NX), other))
-    arrived(keys.at[0, 0], kv_rs.at[4])
-    to_core(keys, 2)
-    arrived(keys.at[0, 0], kv_rs.at[5])
-    to_core(values, 2)
-    unit(6, x_at[2], c)
-    from_core(2)
-    unit(7, x_at[2], other)
-    part, stats = join([parts[n, 129:130] for n in range(8)], [parts[n] for n in range(8)])
+    q_swap = swap(q_line, q_other, 0)
+    q_swap.start()
+    unit(0, x, (0,))
+    q_swap.wait_recv()
+    unit(0, x, (1,))
+    arrived(keys.at[0], kv_rs.at[2])
+    arrived(keys.at[0], kv_rs.at[3])
+    loop(0, 2, lambda i: unit(1 + i, lax.rem(x + 3 - 2 * i, NX), (0, 1)))
+    far = x_at[2]
+    arrived(keys.at[0, pl.ds(256, 512)], kv_rs.at[4])
+    arrived(keys.at[0, pl.ds(256, 512)], kv_rs.at[5])
+    flipped = with_ones(values[far, 256:768])
+    for r in (1, 0):
+        keep(parts.at[r, 3], *join(*zip(store_block(far, flipped, r))))
+    arrived(keys.at[0, pl.ds(0, 256)], kv_rs.at[6])
+    arrived(keys.at[0, pl.ds(0, 256)], kv_rs.at[7])
+    flipped = with_ones(values[far, 0:256])
+    keep(p_send, *joined(1, [prefix_block(far, flipped, 1)]))
+    p_swap = swap(p_send, p_recv, 1)
+    p_swap.start()
+    part, stats = joined(0, [prefix_block(far, flipped, 0)])
+    p_swap.wait_recv()
+    part, stats = join([stats[1:2], p_recv[129:130]], [jnp.concatenate([part, stats], axis=0), p_recv[...]])
 
     by_row = jnp.transpose(part)
     for t in range(NZ):
@@ -293,8 +316,10 @@
         remote(z_send.at[to], z_recv.at[z], z_ss, z_rs, x_to[0] + to, y, c).start()
     z_recv[z] = z_send[z]
     left(q_line.at[pl.ds(0, NZ - 1)], q_ss)
-    left(keys.at[pl.ds(0, 3)], kv_ss)
-    left(keys, fw_ss)
+    left(keys.at[pl.ds(0, 3)], kv_ss.at[0])
+    left(keys.at[pl.ds(0, 3)], kv_ss.at[1])
+    q_swap.wait_send()
+    p_swap.wait_send()
     weights_swap.wait()
     pl.semaphore_wait(col_sem, 2)
     arrived(z_recv.at[pl.ds(0, NZ - 1)], z_rs)
@@ -359,21 +384,26 @@
 ):
     anywhere = pl.BlockSpec(memory_space=pl.ANY)
     vmem = pl.BlockSpec(memory_space=pltpu.VMEM)
-    smem = pl.BlockSpec(memory_space=pltpu.SMEM)
     dma = pltpu.SemaphoreType.DMA
     return pl.pallas_call(
         kernel,
         out_shape=jax.ShapeDtypeStruct((16, 2, 80), F32),
-        in_specs=[anywhere] * 8 + [vmem] * 3 + [smem] * 3,
+        in_specs=[anywhere] * 8 + [vmem] * 3 + [anywhere] * 3,
         out_specs=vmem,
         scratch_shapes=[
+            pltpu.SMEM((16,), jnp.int32),
+            pltpu.SMEM((16,), jnp.int32),
+            pltpu.SMEM((2,), jnp.int32),
             pltpu.VMEM((NZ, ROWS, HD), BF16),
-            pltpu.VMEM((NX, 2, 768, HD), BF16),
-            pltpu.VMEM((NX, 2, 768, HD), BF16),
+            pltpu.VMEM((NZ, ROWS, HD), BF16),
+            pltpu.VMEM((NX, 768, HD), BF16),
+            pltpu.VMEM((NX, 768, HD), BF16),
             pltpu.VMEM((2, 256, HD), BF16),
             pltpu.VMEM((2, 256, HD), BF16),
             pltpu.VMEM((2, 128, 1024), BF16),
-            pltpu.VMEM((8, 136, 256), F32),
+            pltpu.VMEM((2, 4, 136, 256), F32),
+            pltpu.VMEM((136, 256), F32),
+            pltpu.VMEM((136, 256), F32),
             pltpu.VMEM((NZ, 34, 128), F32),
             pltpu.VMEM((NZ, 34, 128), F32),
             pltpu.VMEM((CHIPS, ROWS, HD), BF16),
@@ -381,13 +411,13 @@
             pltpu.VMEM((128, 1024), BF16),
             pltpu.VMEM((2, NY, 16, 128), F32),
             pltpu.VMEM((16, 16, 128), F32),
+            dma((11,)),
+            dma,
+            dma,
+            dma((2,)),
             dma((8,)),
-            dma,
-            dma,
-            dma,
-            dma((6,)),
-            dma,
-            dma((NX,)),
+            dma((2,)),
+            dma((2,)),
             pltpu.SemaphoreType.REGULAR,
             dma,
             dma((2,)),

time: 53.5 us -> 52.7 us (0.985)
  Pallas kernels: 52 us -> 51.2 us
    pallas_call x1, Pallas kernels: 52 us -> 51.2 us  [body(): pl.pallas_call(kernel, out_shape=jax.ShapeDtypeStruct((16, 2, 80), F32),...]
where the time goes in v6:
time: 52.7 us; the launch traced here: 52.5 us
  Pallas kernels  51.2 us (97%)
  local copies, waits for them, and re-layouts  1.33 us (3%)
    pallas_call x1, Pallas kernels, body(): pl.pallas_call(kernel, out_shape=jax.ShapeDtypeStruct((16, 2, 80), F32),...  51.2 us
    unnamed x15, local copies, waits for them, and re-layouts  1.33 us

profile of v6, /device:TPU:1, one launch (start us, length us, event | category | flops | bytes accessed | tf_op | source)
XLA Modules:
  0.0 52.5 jit_solution(1072193678878253361)
XLA Ops:
  0.0 0.0 copy-start
  0.0 0.0 copy-start.6
  0.0 0.0 copy-start.2
  0.0 0.0 copy-start.4
  0.0 0.0 copy-start.5
  0.0 0.0 copy-start.1
  0.0 0.0 copy-start.3
  0.0 0.6 %copy-done = bf16[2,2,8,128]{3,2,1,0:T(8,128)(2,1)S(1)} copy-done((bf16[2,2,8,128]{3,2,1,0:T(8,128)(2,1)S(1)}, bf16[2,2,8,128]{3,2,1,0:T(8,128)(2,1)}, u32[]{:S(2)}) %copy-start) | copy-done | bytes 8216
  0.7 0.0 copy-done.6
  0.7 0.0 copy-done.2
  0.7 0.0 copy-done.4
  0.7 0.0 copy-done.5
  0.7 0.0 copy-done.1
  0.8 0.0 copy-done.3
  0.8 51.2 %shard_map.136 = f32[16,2,80]{2,1,0:T(2,128)S(1)} custom-call(bf16[32,128]{1,0:T(8,128)(2,1)S(1)} %bitcast.11, bf16[256,128]{1,0:T(8,128)(2,1)} %bitcast.20, bf16[256,128]{1,0:T(8,128)(2,1)} %bitcast.21, bf16[512,128]{1,0:T(8,128)(2,1)} %bitcast.16, bf16[512,128]{1,0:T(8,128)(2,1)} %bitcast.17, bf16[2,256,128]{2,1,0:T(8,128)(2,1)} %bitcast.18, ...), custom_call_target="tpu_custom_call" | custom-call | tf_op jit(solution)/shard_map/pallas_call | solution.py:388
  51.9 0.6 %copy.16 = f32[16,2,80]{2,1,0:T(2,128)} copy(f32[16,2,80]{2,1,0:T(2,128)S(1)} %shard_map.136) | data formatting | bytes 20480
Async XLA Ops:
  0.0 0.7 %copy-start = (bf16[2,2,8,128]{3,2,1,0:T(8,128)(2,1)S(1)}, bf16[2,2,8,128]{3,2,1,0:T(8,128)(2,1)}, u32[]{:S(2)}) copy-start(bf16[2,2,8,128]{3,2,1,0:T(8,128)(2,1)} %param.14) | copy-start | bytes 24580
  0.0 0.7 %copy-start.6 = (s32[2]{0:T(128)S(1)}, s32[2]{0:T(128)}, u32[]{:S(2)}) copy-start(s32[2]{0:T(128)} %cont_len_in.1) | copy-start | bytes 28
  0.0 0.7 %copy-start.2 = (bf16[2,2,1,128]{3,1,2,0:T(2,128)(2,1)S(1)}, bf16[2,2,1,128]{3,1,2,0:T(2,128)(2,1)}, u32[]{:S(2)}) copy-start(bf16[2,2,1,128]{3,1,2,0:T(2,128)(2,1)} %param.16) | copy-start | bytes 3076
  0.0 0.7 %copy-start.4 = (s32[16]{0:T(128)S(1)}, s32[16]{0:T(128)}, u32[]{:S(2)}) copy-start(s32[16]{0:T(128)} %group_prompt_in.1) | copy-start | bytes 196
  0.0 0.7 %copy-start.5 = (s32[16]{0:T(128)S(1)}, s32[16]{0:T(128)}, u32[]{:S(2)}) copy-start(s32[16]{0:T(128)} %prompt_len_in.1) | copy-start | bytes 196
  0.0 0.7 %copy-start.1 = (bf16[2,2,1,128]{3,1,2,0:T(2,128)(2,1)S(1)}, bf16[2,2,1,128]{3,1,2,0:T(2,128)(2,1)}, u32[]{:S(2)}) copy-start(bf16[2,2,1,128]{3,1,2,0:T(2,128)(2,1)} %param.15) | copy-start | bytes 3076
  0.0 0.7 %copy-start.3 = (s32[128]{0:T(128)S(1)}, s32[128]{0:T(128)}, u32[]{:S(2)}) copy-start(s32[128]{0:T(128)} %param.25) | copy-start | bytes 1540

commit v7 on v6

--- a/solution.py
+++ b/solution.py
@@ -144,9 +144,8 @@
         greet(x_to[dx] + z, y, c)
     for dz in (2, 6, 1, 7):
         greet(x_to[0] + z_to[dz], y, c)
-    for dy in (2, 6, 1, 7):
+    for dy in (1, 7):
         greet(chip, y_to[dy], c)
-        greet(chip, y_to[dy], other)
     greet(chip, y, other)
 
     local = [
@@ -167,9 +166,7 @@
             ]
         )
     ]
-    for copy in local:
-        copy.start()
-    pl.semaphore_wait(barrier, 15)
+    pl.semaphore_wait(barrier, 9)
 
     def arrived(ref, sem):
         remote(ref, ref, q_ss, sem, chip, y, other).wait_recv()
@@ -199,6 +196,8 @@
     own_to_x(pv_in, sv_in, values, 1, 3)
     for dz in (2, 6, 1, 7):
         q_send(0, 0, dz)
+    for copy in local:
+        copy.start()
     own_to_x(pv_in, sv_in, values, 3, 1)
     own_to_x(pk_in, sk_in, keys, 2, 3)
     for copy in local:
@@ -207,8 +206,8 @@
         wt.at[c, pl.ds(0, 80)], wt.at[c, pl.ds(0, 80)], w_ss, w_rs, chip, y, other
     )
     weights_swap.start()
-    for dy in (2, 6):
-        greet(chip, y_to[dy], c, col_sem)
+    for dy in (1, 7):
+        greet(chip, y_to[dy], c, col_sem.at[0])
 
     wt[:, 80:, :] = jnp.zeros((2, 48, wt.shape[2]), BF16)
     lane = iota((128, 256), 1)
@@ -267,9 +266,9 @@
             blocks = [prefix_block(at, flipped[:, :256], r), store_block(at, flipped[:, 256:], r)]
             keep(parts.at[r, n], *join(*zip(*blocks)))
 
-    def joined(r, more):
-        kept = [(parts[r, n, 129:130], parts[r, n]) for n in range(4)]
-        return join(*zip(*(kept + more)))
+    def joined(r, slots, block):
+        kept = [(parts[r, n, 129:130], parts[r, n]) for n in slots]
+        return join(*zip(*(kept + [block])))
 
     arrived(q_line.at[pl.ds(0, 4)], q_rs.at[0])
     q_send(1, 1, 6)
@@ -285,6 +284,9 @@
     unit(0, x, (0,))
     q_swap.wait_recv()
     unit(0, x, (1,))
+    pl.semaphore_wait(col_sem.at[0], 2)
+    for dy in (2, 6):
+        greet(chip, y_to[dy], c, col_sem.at[1])
     arrived(keys.at[0], kv_rs.at[2])
     arrived(keys.at[0], kv_rs.at[3])
     loop(0, 2, lambda i: unit(1 + i, lax.rem(x + 3 - 2 * i, NX), (0, 1)))
@@ -293,14 +295,15 @@
     arrived(keys.at[0, pl.ds(256, 512)], kv_rs.at[5])
     flipped = with_ones(values[far, 256:768])
     for r in (1, 0):
-        keep(parts.at[r, 3], *join(*zip(store_block(far, flipped, r))))
+        keep(parts.at[r, 3], *joined(r, (0, 1, 2), store_block(far, flipped, r)))
     arrived(keys.at[0, pl.ds(0, 256)], kv_rs.at[6])
     arrived(keys.at[0, pl.ds(0, 256)], kv_rs.at[7])
     flipped = with_ones(values[far, 0:256])
-    keep(p_send, *joined(1, [prefix_block(far, flipped, 1)]))
+    keep(p_send, *joined(1, (3,), prefix_block(far, flipped, 1)))
     p_swap = swap(p_send, p_recv, 1)
+    pl.semaphore_wait(col_sem.at[1], 2)
     p_swap.start()
-    part, stats = joined(0, [prefix_block(far, flipped, 0)])
+    part, stats = joined(0, (3,), prefix_block(far, flipped, 0))
     p_swap.wait_recv()
     part, stats = join([stats[1:2], p_recv[129:130]], [jnp.concatenate([part, stats], axis=0), p_recv[...]])
 
@@ -321,7 +324,6 @@
     q_swap.wait_send()
     p_swap.wait_send()
     weights_swap.wait()
-    pl.semaphore_wait(col_sem, 2)
     arrived(z_recv.at[pl.ds(0, NZ - 1)], z_rs)
 
     side = jnp.concatenate(
@@ -340,17 +342,28 @@
         weighted = weighted + factor * z_recv[s, 0:ROWS]
     att[chip] = (weighted / total).astype(BF16)
 
-    for dx, dz in FAR_FIRST:
+    def a_copy(dx, to_z):
         block = att.at[chip]
-        remote(block, block, a_ss, a_rs, x_to[dx] + z_to[dz], y, c).start()
+        return remote(block, block, a_ss, a_rs.at[dx], x_to[dx] + to_z, y, c)
+
+    for to_z in range(NZ):
+        for dx in X_STEPS[:-1]:
+            a_copy(dx, to_z).start()
+
+        @pl.when(to_z != z)
+        def _():
+            a_copy(0, to_z).start()
+
     left(z_send.at[pl.ds(0, NZ - 1)], z_ss)
-    arrived(att.at[pl.ds(0, CHIPS - 1)], a_rs)
-
-    att_f32[...] = att[...].reshape(CHIPS * ROWS, HD).astype(F32)
-    for h in range(GROUP):
-        flat[:, h * HD : (h + 1) * HD] = att_f32[pl.ds(h, 128, stride=GROUP), :].astype(BF16)
+    for d in (0, 1, 3, 2):
+        arrived(att.at[pl.ds(0, NZ if d else NZ - 1)], a_rs.at[d])
+        at = x_at[(NX - d) % NX]
+        att_f32[...] = att[pl.ds(at * NZ, NZ)].reshape(NZ * ROWS, HD).astype(F32)
+        for h in range(GROUP):
+            tokens = att_f32[pl.ds(h, 32, stride=GROUP), :]
+            flat[at, :, h * HD : (h + 1) * HD] = tokens.astype(BF16)
     for to_c in (other, c):
-        y_send[to_c] = dot_nt(flat[...], wt[to_c]).reshape(NY, 16, 128)
+        y_send[to_c] = dot_nt(flat[...].reshape(128, 1024), wt[to_c]).reshape(NY, 16, 128)
         for dy in Y_STEPS if to_c is other else Y_STEPS[:-1]:
             to_y = y_to[dy]
             remote(y_send.at[to_c, to_y], y_recv.at[yc], y_ss, y_rs, chip, to_y, to_c).start()
@@ -407,8 +420,8 @@
             pltpu.VMEM((NZ, 34, 128), F32),
             pltpu.VMEM((NZ, 34, 128), F32),
             pltpu.VMEM((CHIPS, ROWS, HD), BF16),
-            pltpu.VMEM((CHIPS * ROWS, HD), F32),
-            pltpu.VMEM((128, 1024), BF16),
+            pltpu.VMEM((NZ * ROWS, HD), F32),
+            pltpu.VMEM((NX, 32, 1024), BF16),
             pltpu.VMEM((2, NY, 16, 128), F32),
             pltpu.VMEM((16, 16, 128), F32),
             dma((11,)),
@@ -418,13 +431,13 @@
             dma((8,)),
             dma((2,)),
             dma((2,)),
-            pltpu.SemaphoreType.REGULAR,
+            pltpu.SemaphoreType.REGULAR((2,)),
             dma,
             dma((2,)),
             dma,
             dma,
             dma,
-            dma,
+            dma((NX,)),
             dma,
             dma,
         ],

time: 52.7 us -> 51.5 us (0.977)
  Pallas kernels: 51.2 us -> 49.7 us
    pallas_call x1, Pallas kernels: 51.2 us -> 49.7 us  [body(): pl.pallas_call(kernel, out_shape=jax.ShapeDtypeStruct((16, 2, 80), F32),...]
where the time goes in v7:
time: 51.5 us; the launch traced here: 51.1 us
  Pallas kernels  49.7 us (97%)
  local copies, waits for them, and re-layouts  1.33 us (3%)
    pallas_call x1, Pallas kernels, body(): pl.pallas_call(kernel, out_shape=jax.ShapeDtypeStruct((16, 2, 80), F32),...  49.7 us
    unnamed x15, local copies, waits for them, and re-layouts  1.33 us

profile of v7, /device:TPU:1, one launch (start us, length us, event | category | flops | bytes accessed | tf_op | source)
XLA Modules:
  0.0 51.1 jit_solution(1097845247211876960)
XLA Ops:
  0.0 0.0 copy-start
  0.0 0.0 copy-start.6
  0.0 0.0 copy-start.2
  0.0 0.0 copy-start.4
  0.0 0.0 copy-start.5
  0.0 0.0 copy-start.1
  0.0 0.0 copy-start.3
  0.0 0.6 %copy-done = bf16[2,2,8,128]{3,2,1,0:T(8,128)(2,1)S(1)} copy-done((bf16[2,2,8,128]{3,2,1,0:T(8,128)(2,1)S(1)}, bf16[2,2,8,128]{3,2,1,0:T(8,128)(2,1)}, u32[]{:S(2)}) %copy-start) | copy-done | bytes 8216
  0.7 0.0 copy-done.6
  0.7 0.0 copy-done.2
  0.7 0.0 copy-done.4
  0.7 0.0 copy-done.5
  0.7 0.0 copy-done.1
  0.8 0.0 copy-done.3
  0.8 49.7 %shard_map.136 = f32[16,2,80]{2,1,0:T(2,128)S(1)} custom-call(bf16[32,128]{1,0:T(8,128)(2,1)S(1)} %bitcast.11, bf16[256,128]{1,0:T(8,128)(2,1)} %bitcast.20, bf16[256,128]{1,0:T(8,128)(2,1)} %bitcast.21, bf16[512,128]{1,0:T(8,128)(2,1)} %bitcast.16, bf16[512,128]{1,0:T(8,128)(2,1)} %bitcast.17, bf16[2,256,128]{2,1,0:T(8,128)(2,1)} %bitcast.18, ...), custom_call_target="tpu_custom_call" | custom-call | tf_op jit(solution)/shard_map/pallas_call | solution.py:401
  50.5 0.6 %copy.16 = f32[16,2,80]{2,1,0:T(2,128)} copy(f32[16,2,80]{2,1,0:T(2,128)S(1)} %shard_map.136) | data formatting | bytes 20480
Async XLA Ops:
  0.0 0.7 %copy-start = (bf16[2,2,8,128]{3,2,1,0:T(8,128)(2,1)S(1)}, bf16[2,2,8,128]{3,2,1,0:T(8,128)(2,1)}, u32[]{:S(2)}) copy-start(bf16[2,2,8,128]{3,2,1,0:T(8,128)(2,1)} %param.14) | copy-start | bytes 24580
  0.0 0.7 %copy-start.6 = (s32[2]{0:T(128)S(1)}, s32[2]{0:T(128)}, u32[]{:S(2)}) copy-start(s32[2]{0:T(128)} %cont_len_in.1) | copy-start | bytes 28
  0.0 0.7 %copy-start.2 = (bf16[2,2,1,128]{3,1,2,0:T(2,128)(2,1)S(1)}, bf16[2,2,1,128]{3,1,2,0:T(2,128)(2,1)}, u32[]{:S(2)}) copy-start(bf16[2,2,1,128]{3,1,2,0:T(2,128)(2,1)} %param.16) | copy-start | bytes 3076
  0.0 0.7 %copy-start.4 = (s32[16]{0:T(128)S(1)}, s32[16]{0:T(128)}, u32[]{:S(2)}) copy-start(s32[16]{0:T(128)} %group_prompt_in.1) | copy-start | bytes 196
  0.0 0.7 %copy-start.5 = (s32[16]{0:T(128)S(1)}, s32[16]{0:T(128)}, u32[]{:S(2)}) copy-start(s32[16]{0:T(128)} %prompt_len_in.1) | copy-start | bytes 196
  0.0 0.7 %copy-start.1 = (bf16[2,2,1,128]{3,1,2,0:T(2,128)(2,1)S(1)}, bf16[2,2,1,128]{3,1,2,0:T(2,128)(2,1)}, u32[]{:S(2)}) copy-start(bf16[2,2,1,128]{3,1,2,0:T(2,128)(2,1)} %param.15) | copy-start | bytes 3076
  0.0 0.7 %copy-start.3 = (s32[128]{0:T(128)S(1)}, s32[128]{0:T(128)}, u32[]{:S(2)}) copy-start(s32[128]{0:T(128)} %param.25) | copy-start | bytes 1540

commit v8 on v7

--- a/solution.py
+++ b/solution.py
@@ -355,6 +355,24 @@
             a_copy(0, to_z).start()
 
     left(z_send.at[pl.ds(0, NZ - 1)], z_ss)
+
+    def project(at):
+        for to_c in (other, c):
+            y_send[to_c, pl.ds(at * 2, 2)] = dot_nt(flat[at], wt[to_c]).reshape(2, 16, 128)
+        for to_y in (at * 2, at * 2 + 1):
+            y_copy(to_y, other).start()
+
+            @pl.when(to_y != y)
+            def _():
+                y_copy(to_y, c).start()
+
+            @pl.when(to_y == y)
+            def _():
+                y_recv[yc] = y_send[c, to_y]
+
+    def y_copy(to_y, to_c):
+        return remote(y_send.at[to_c, to_y], y_recv.at[yc], y_ss, y_rs, chip, to_y, to_c)
+
     for d in (0, 1, 3, 2):
         arrived(att.at[pl.ds(0, NZ if d else NZ - 1)], a_rs.at[d])
         at = x_at[(NX - d) % NX]
@@ -362,12 +380,7 @@
         for h in range(GROUP):
             tokens = att_f32[pl.ds(h, 32, stride=GROUP), :]
             flat[at, :, h * HD : (h + 1) * HD] = tokens.astype(BF16)
-    for to_c in (other, c):
-        y_send[to_c] = dot_nt(flat[...].reshape(128, 1024), wt[to_c]).reshape(NY, 16, 128)
-        for dy in Y_STEPS if to_c is other else Y_STEPS[:-1]:
-            to_y = y_to[dy]
-            remote(y_send.at[to_c, to_y], y_recv.at[yc], y_ss, y_rs, chip, to_y, to_c).start()
-    y_recv[yc] = y_send[c, y]
+        project(at)
     left(att.at[pl.ds(0, CHIPS - 1)], a_ss)
     arrived(y_recv.at[pl.ds(0, 15)], y_rs)
     for b in range(2):

time: 51.5 us -> 51.2 us (level)
  no operation moved by 1% of the time
where the time goes in v8:
time: 51.2 us; the launch traced here: 51 us
  Pallas kernels  49.7 us (97%)
  local copies, waits for them, and re-layouts  1.33 us (3%)
    pallas_call x1, Pallas kernels, body(): pl.pallas_call(kernel, out_shape=jax.ShapeDtypeStruct((16, 2, 80), F32),...  49.7 us
    unnamed x15, local copies, waits for them, and re-layouts  1.33 us

profile of v8, /device:TPU:1, one launch (start us, length us, event | category | flops | bytes accessed | tf_op | source)
XLA Modules:
  0.0 51.0 jit_solution(17145378036741597285)
XLA Ops:
  0.0 0.0 copy-start
  0.0 0.0 copy-start.6
  0.0 0.0 copy-start.2
  0.0 0.0 copy-start.4
  0.0 0.0 copy-start.5
  0.0 0.0 copy-start.1
  0.0 0.0 copy-start.3
  0.0 0.6 %copy-done = bf16[2,2,8,128]{3,2,1,0:T(8,128)(2,1)S(1)} copy-done((bf16[2,2,8,128]{3,2,1,0:T(8,128)(2,1)S(1)}, bf16[2,2,8,128]{3,2,1,0:T(8,128)(2,1)}, u32[]{:S(2)}) %copy-start) | copy-done | bytes 8216
  0.7 0.0 copy-done.6
  0.7 0.0 copy-done.2
  0.7 0.0 copy-done.4
  0.7 0.0 copy-done.5
  0.7 0.0 copy-done.1
  0.8 0.0 copy-done.3
  0.8 49.7 %shard_map.136 = f32[16,2,80]{2,1,0:T(2,128)S(1)} custom-call(bf16[32,128]{1,0:T(8,128)(2,1)S(1)} %bitcast.11, bf16[256,128]{1,0:T(8,128)(2,1)} %bitcast.20, bf16[256,128]{1,0:T(8,128)(2,1)} %bitcast.21, bf16[512,128]{1,0:T(8,128)(2,1)} %bitcast.16, bf16[512,128]{1,0:T(8,128)(2,1)} %bitcast.17, bf16[2,256,128]{2,1,0:T(8,128)(2,1)} %bitcast.18, ...), custom_call_target="tpu_custom_call" | custom-call | tf_op jit(solution)/shard_map/pallas_call | solution.py:414
  50.4 0.6 %copy.16 = f32[16,2,80]{2,1,0:T(2,128)} copy(f32[16,2,80]{2,1,0:T(2,128)S(1)} %shard_map.136) | data formatting | bytes 20480
Async XLA Ops:
  0.0 0.7 %copy-start = (bf16[2,2,8,128]{3,2,1,0:T(8,128)(2,1)S(1)}, bf16[2,2,8,128]{3,2,1,0:T(8,128)(2,1)}, u32[]{:S(2)}) copy-start(bf16[2,2,8,128]{3,2,1,0:T(8,128)(2,1)} %param.14) | copy-start | bytes 24580
  0.0 0.7 %copy-start.6 = (s32[2]{0:T(128)S(1)}, s32[2]{0:T(128)}, u32[]{:S(2)}) copy-start(s32[2]{0:T(128)} %cont_len_in.1) | copy-start | bytes 28
  0.0 0.7 %copy-start.2 = (bf16[2,2,1,128]{3,1,2,0:T(2,128)(2,1)S(1)}, bf16[2,2,1,128]{3,1,2,0:T(2,128)(2,1)}, u32[]{:S(2)}) copy-start(bf16[2,2,1,128]{3,1,2,0:T(2,128)(2,1)} %param.16) | copy-start | bytes 3076
  0.0 0.7 %copy-start.4 = (s32[16]{0:T(128)S(1)}, s32[16]{0:T(128)}, u32[]{:S(2)}) copy-start(s32[16]{0:T(128)} %group_prompt_in.1) | copy-start | bytes 196
  0.0 0.7 %copy-start.5 = (s32[16]{0:T(128)S(1)}, s32[16]{0:T(128)}, u32[]{:S(2)}) copy-start(s32[16]{0:T(128)} %prompt_len_in.1) | copy-start | bytes 196
  0.0 0.7 %copy-start.1 = (bf16[2,2,1,128]{3,1,2,0:T(2,128)(2,1)S(1)}, bf16[2,2,1,128]{3,1,2,0:T(2,128)(2,1)}, u32[]{:S(2)}) copy-start(bf16[2,2,1,128]{3,1,2,0:T(2,128)(2,1)} %param.15) | copy-start | bytes 3076
  0.0 0.7 %copy-start.3 = (s32[128]{0:T(128)S(1)}, s32[128]{0:T(128)}, u32[]{:S(2)}) copy-start(s32[128]{0:T(128)} %param.25) | copy-start | bytes 1540

commit v9 on v8

--- a/solution.py
+++ b/solution.py
@@ -347,13 +347,11 @@
         return remote(block, block, a_ss, a_rs.at[dx], x_to[dx] + to_z, y, c)
 
     for to_z in range(NZ):
-        for dx in X_STEPS[:-1]:
-            a_copy(dx, to_z).start()
-
-        @pl.when(to_z != z)
-        def _():
-            a_copy(0, to_z).start()
-
+        for to_x in (0, 1, 3, 2):
+            dx = lax.rem(to_x - x + NX, NX)
+            block = att.at[chip]
+            copy = remote(block, block, a_ss, a_rs.at[dx], to_x * NZ + to_z, y, c)
+            pl.when((to_z != z) | (to_x != x))(copy.start)
     left(z_send.at[pl.ds(0, NZ - 1)], z_ss)
 
     def project(at):

time: 51.2 us -> 50.6 us (0.988); the launches traced: 51 us -> 49.8 us
  Pallas kernels: 49.7 us -> 48.4 us
    pallas_call x1, Pallas kernels: 49.7 us -> 48.4 us  [body(): pl.pallas_call(kernel, out_shape=jax.ShapeDtypeStruct((16, 2, 80), F32),...]
where the time goes in v9:
time: 50.6 us; the launch traced here: 49.8 us
  Pallas kernels  48.4 us (96%)
  local copies, waits for them, and re-layouts  1.33 us (3%)
    pallas_call x1, Pallas kernels, body(): pl.pallas_call(kernel, out_shape=jax.ShapeDtypeStruct((16, 2, 80), F32),...  48.4 us
    unnamed x15, local copies, waits for them, and re-layouts  1.33 us

profile of v9, /device:TPU:1, one launch (start us, length us, event | category | flops | bytes accessed | tf_op | source)
XLA Modules:
  0.0 49.8 jit_solution(3132491780665520121)
XLA Ops:
  0.0 0.0 copy-start
  0.0 0.0 copy-start.6
  0.0 0.0 copy-start.2
  0.0 0.0 copy-start.4
  0.0 0.0 copy-start.5
  0.0 0.0 copy-start.1
  0.0 0.0 copy-start.3
  0.0 0.6 %copy-done = bf16[2,2,8,128]{3,2,1,0:T(8,128)(2,1)S(1)} copy-done((bf16[2,2,8,128]{3,2,1,0:T(8,128)(2,1)S(1)}, bf16[2,2,8,128]{3,2,1,0:T(8,128)(2,1)}, u32[]{:S(2)}) %copy-start) | copy-done | bytes 8216
  0.7 0.0 copy-done.6
  0.7 0.0 copy-done.2
  0.7 0.0 copy-done.4
  0.7 0.0 copy-done.5
  0.7 0.0 copy-done.1
  0.8 0.0 copy-done.3
  0.8 48.4 %shard_map.136 = f32[16,2,80]{2,1,0:T(2,128)S(1)} custom-call(bf16[32,128]{1,0:T(8,128)(2,1)S(1)} %bitcast.11, bf16[256,128]{1,0:T(8,128)(2,1)} %bitcast.20, bf16[256,128]{1,0:T(8,128)(2,1)} %bitcast.21, bf16[512,128]{1,0:T(8,128)(2,1)} %bitcast.16, bf16[512,128]{1,0:T(8,128)(2,1)} %bitcast.17, bf16[2,256,128]{2,1,0:T(8,128)(2,1)} %bitcast.18, ...), custom_call_target="tpu_custom_call" | custom-call | tf_op jit(solution)/shard_map/pallas_call | solution.py:412
  49.1 0.6 %copy.16 = f32[16,2,80]{2,1,0:T(2,128)} copy(f32[16,2,80]{2,1,0:T(2,128)S(1)} %shard_map.136) | data formatting | bytes 20480
Async XLA Ops:
  0.0 0.7 %copy-start = (bf16[2,2,8,128]{3,2,1,0:T(8,128)(2,1)S(1)}, bf16[2,2,8,128]{3,2,1,0:T(8,128)(2,1)}, u32[]{:S(2)}) copy-start(bf16[2,2,8,128]{3,2,1,0:T(8,128)(2,1)} %param.14) | copy-start | bytes 24580
  0.0 0.7 %copy-start.6 = (s32[2]{0:T(128)S(1)}, s32[2]{0:T(128)}, u32[]{:S(2)}) copy-start(s32[2]{0:T(128)} %cont_len_in.1) | copy-start | bytes 28
  0.0 0.7 %copy-start.2 = (bf16[2,2,1,128]{3,1,2,0:T(2,128)(2,1)S(1)}, bf16[2,2,1,128]{3,1,2,0:T(2,128)(2,1)}, u32[]{:S(2)}) copy-start(bf16[2,2,1,128]{3,1,2,0:T(2,128)(2,1)} %param.16) | copy-start | bytes 3076
  0.0 0.7 %copy-start.4 = (s32[16]{0:T(128)S(1)}, s32[16]{0:T(128)}, u32[]{:S(2)}) copy-start(s32[16]{0:T(128)} %group_prompt_in.1) | copy-start | bytes 196
  0.0 0.7 %copy-start.5 = (s32[16]{0:T(128)S(1)}, s32[16]{0:T(128)}, u32[]{:S(2)}) copy-start(s32[16]{0:T(128)} %prompt_len_in.1) | copy-start | bytes 196
  0.0 0.7 %copy-start.1 = (bf16[2,2,1,128]{3,1,2,0:T(2,128)(2,1)S(1)}, bf16[2,2,1,128]{3,1,2,0:T(2,128)(2,1)}, u32[]{:S(2)}) copy-start(bf16[2,2,1,128]{3,1,2,0:T(2,128)(2,1)} %param.15) | copy-start | bytes 3076
  0.0 0.7 %copy-start.3 = (s32[128]{0:T(128)S(1)}, s32[128]{0:T(128)}, u32[]{:S(2)}) copy-start(s32[128]{0:T(128)} %param.25) | copy-start | bytes 1540
